TPU v7x, 128 devices: a whole 4x4x4 slice. The times are simulated.
128 devices in a mesh: prompt: 16 (over y, z), resp: 8 (over x, core).
Axes of the slice: x: 4, y: 4, z: 4, core: 2. Of those that a mesh axis runs over, the one named last changes fastest.
Arguments:
- queries: bfloat16 [16, 8, 16, 16, 5120], P('prompt', 'resp'), may hold values from -80 to 80
- grad_out: bfloat16 [16, 8, 16, 16, 5120], P('prompt', 'resp'), may hold values from -6 to 6
- response_keys: bfloat16 [16, 8, 16, 16, 1024], P('prompt', 'resp'), may hold values from -4 to 4
- response_values: bfloat16 [16, 8, 16, 16, 1024], P('prompt', 'resp'), may hold values from -6 to 6
- prompt_prefix_keys: bfloat16 [16, 384, 1024], P('prompt', 'resp'), may hold values from -6 to 6
- prompt_prefix_values: bfloat16 [16, 384, 1024], P('prompt', 'resp'), may hold values from -6 to 6
- lengths: int32 [16, 8, 16], P('prompt', 'resp'), may hold values from 1 to 16, 160 in all within a row
- prompt_of: int32 [16, 8, 16], P('prompt', 'resp'), may hold values from 0 to 15, each once within a row
Outputs:
- attn_out: bfloat16 [16, 8, 16, 16, 5120], P('prompt', 'resp')
- query_grads: bfloat16 [16, 8, 16, 16, 5120], P('prompt', 'resp')
- resp_key_grads: bfloat16 [16, 8, 16, 16, 1024], P('prompt', 'resp')
- resp_value_grads: bfloat16 [16, 8, 16, 16, 1024], P('prompt', 'resp')
- prefix_key_grads: float32 [16, 384, 1024], P('prompt', 'resp')
- prefix_value_grads: float32 [16, 384, 1024], P('prompt', 'resp')
Inputs may be any that keep to these rules, and one draw needn't show every extreme that they name: `prompt_of`: on every device the 16 responses answer 16 different prompts. On every device the lengths sum to 160 and the longest is 16.
All inputs are finite; a program needn't handle non-finite values.
Results may differ from a plain program's by a relative error of at most 0.017.
Values may be sent and summed in bfloat16 or wider, within the bound.
A program may use at most 192 MiB of HBM per device.

v0:
```python
import jax
import jax.numpy as jnp
from jax import lax
from jax.experimental import pallas as pl
from jax.experimental.pallas import tpu as pltpu
from jax.sharding import PartitionSpec as P

KEY_HEADS = 8
WIDTH = 128
GROUP = 5
SLOTS = 16
RESPONSES = 16
TOKENS = SLOTS * RESPONSES
LIVE = 160
PREFIX = 384
SIDE = 4
ROWS = PREFIX // 8
PIECE = 2 * PREFIX
GW = GROUP * WIDTH
MSG = 2 * GW + 2 * WIDTH
MESH = pl.DeviceIdType.MESH
BF16 = jnp.bfloat16
F32 = jnp.float32
SCALE = WIDTH**-0.5
EXP2_SCALE = SCALE * 1.4426950408889634
VMEM_LIMIT = 58 * 1024 * 1024


class Place:
    def __init__(self):
        prompt, resp = lax.axis_index("prompt"), lax.axis_index("resp")
        self.y, self.z = prompt // SIDE, prompt % SIDE
        self.x, self.c = resp // 2, resp % 2
        self.prompt, self.resp = prompt, resp
        x, y, z, c = self.x, self.y, self.z, self.c
        self.sibling = (prompt, x * 2 + 1 - c)
        self.home_slot = 2 * (x * (1 - c) + y * c) + c
        self.head = x * (1 - c) + (SIDE + y) * c
        self.line = y * (1 - c) + x * c
        self.routes = []
        for k in (2, 1, 3):
            xd, yd = (x + k) % SIDE, (y + k) % SIDE
            self.routes.append((xd, 2 * x + c, (prompt, 2 * xd)))
            self.routes.append((SIDE + yd, 2 * y + c, (yd * SIDE + z, 2 * x + 1)))
        self.routes.append(((SIDE + y) * (1 - c) + x * c, 2 * y * (1 - c) + (2 * x + 1) * c, self.sibling))
        self.routes.append((self.head, self.home_slot, None))

    def source(self, k, core):
        along = (self.x * (1 - self.c) + self.y * self.c + k) % SIDE
        prompt = self.prompt * (1 - self.c) + (along * SIDE + self.z) * self.c
        resp = (along * 2 + core) * (1 - self.c) + (2 * self.x + core) * self.c
        return 2 * along + core, (prompt, resp)

    def line_peer(self, k):
        prompt = ((self.y + k * (1 - self.c)) % SIDE) * SIDE + self.z
        return (prompt, ((self.x + k * self.c) % SIDE) * 2 + self.c)

    def z_peer(self, k):
        return (self.y * SIDE + (self.z + k) % SIDE, self.resp)

    def barrier(self):
        sem = pltpu.get_barrier_semaphore()
        peers = [self.sibling]
        for k in (1, 2, 3):
            peers.append(self.z_peer(k))
            for core in (0, 1):
                peers.append((self.prompt, ((self.x + k) % SIDE) * 2 + core))
                peers.append((((self.y + k) % SIDE) * SIDE + self.z, 2 * self.x + core))
        for peer in peers:
            pl.semaphore_signal(sem, inc=1, device_id=peer, device_id_type=MESH)
        pl.semaphore_wait(sem, len(peers))


def remote(src, dst, send, recv, device):
    return pltpu.make_async_remote_copy(
        src_ref=src, dst_ref=dst, send_sem=send, recv_sem=recv, device_id=device, device_id_type=MESH
    )


def pack_rows(len_ref, prm_ref):
    lane = lax.broadcasted_iota(jnp.int32, (1, TOKENS), 1)
    response, token = lane >> 4, lane & (SLOTS - 1)
    row = jnp.full((1, TOKENS), -1, jnp.int32)
    slot = jnp.zeros((1, TOKENS), jnp.int32)
    start = jnp.int32(0)
    for j in range(RESPONSES):
        length = len_ref[j]
        mine = response == j
        row = jnp.where(mine & (token < length), start + token, row)
        slot = jnp.where(mine, prm_ref[j] * SLOTS + token, slot)
        start = start + length
    return row, slot


def one_hot_pack(row):
    packed = lax.broadcasted_iota(jnp.int32, (LIVE, TOKENS), 0)
    return jnp.where(packed == row, 1.0, 0.0).astype(BF16)


def dot(a, b, dims):
    return lax.dot_general(a, b, (dims, ((), ())), preferred_element_type=F32)


NN = ((1,), (0,))
NT = ((1,), (1,))
TN = ((0,), (0,))


def scatter_kernel(
    len_ref, prm_ref, q, g, k, v, pk, pv, recv, slots, kv,
    xb, send, slot_send, in_sem, x_send, x_recv, sl_send, sl_recv, a_send, a_recv, b_send, b_recv, c_send, c_recv, own_sem,
):
    me = Place()
    routes = me.routes
    for n, (head, _, _) in enumerate(routes):
        wide = pl.ds(pl.multiple_of(head * GW, WIDTH), GW)
        narrow = pl.ds(pl.multiple_of(head * WIDTH, WIDTH), WIDTH)
        for src, cols, low, size in ((q, wide, 0, GW), (g, wide, GW, GW), (k, narrow, 2 * GW, WIDTH), (v, narrow, 2 * GW + WIDTH, WIDTH)):
            pltpu.make_async_copy(src.at[:, cols], xb.at[n, :, pl.ds(low, size)], in_sem.at[n]).start()
    me.barrier()

    stage_a = []
    for n, (head, _, device) in enumerate(routes):
        narrow = pl.ds(pl.multiple_of(head * WIDTH, WIDTH), WIDTH)
        on_y = head // SIDE
        for i, src in enumerate((pk, pv)):
            piece = me.y * (1 - on_y) + me.x * on_y
            low = (i * PREFIX + me.resp * ROWS) * (1 - on_y) + ((me.y * 2 + i) * 2 * ROWS + me.c * ROWS) * on_y
            dst = kv.at[me.z, piece, pl.ds(pl.multiple_of(low, 16), ROWS)]
            slot = routes[n][1]
            if device is None:
                copy = pltpu.make_async_copy(src.at[:, narrow], dst, own_sem.at[1 + i])
            else:
                copy = remote(src.at[:, narrow], dst, a_send.at[n, i], a_recv.at[slot, i], device)
            copy.start()
            stage_a.append(copy)

    row, slot = pack_rows(len_ref, prm_ref)
    pack = one_hot_pack(row)
    slot8 = jnp.broadcast_to(slot, (8, TOKENS)).astype(F32).astype(BF16)
    slot_send[...] = dot(slot8, pack, NT)
    sent = []
    for n, (_, there, device) in enumerate(routes):
        if device is None:
            copy = pltpu.make_async_copy(slot_send, slots.at[there], own_sem.at[3])
        else:
            copy = remote(slot_send, slots.at[there], sl_send.at[n], sl_recv.at[there], device)
        copy.start()
        sent.append(copy)

    def pack_and_send(n):
        _, there, device = routes[n]
        pltpu.make_async_copy(xb.at[n], xb.at[n], in_sem.at[n]).wait()
        send[n] = dot(pack, xb[n], NN).astype(BF16)
        if device is None:
            copy = pltpu.make_async_copy(send.at[n], recv.at[there], own_sem.at[0])
        else:
            copy = remote(send.at[n], recv.at[there], x_send.at[n], x_recv.at[there], device)
        copy.start()
        sent.append(copy)

    def spread(piece, index):
        for k in (2, 1, 3):
            ref = kv.at[me.z, piece]
            copy = remote(ref, ref, c_send.at[index, k - 1], c_recv.at[index, k - 1], me.z_peer(k))
            copy.start()
            sent.append(copy)

    pack_and_send(0)
    pack_and_send(1)
    for k in range(SIDE):
        for core in (0, 1):
            there, device = me.source(k, core)
            sx = (me.x + k) % SIDE * (1 - me.c) + me.x * me.c
            sy = me.y * (1 - me.c) + (me.y + k) % SIDE * me.c
            piece = sy * (1 - me.c) + sx * me.c
            for i in (0, 1):
                low = (i * PREFIX + (2 * sx + core) * ROWS) * (1 - me.c) + ((sy * 2 + i) * 2 * ROWS + core * ROWS) * me.c
                dst = kv.at[me.z, piece, pl.ds(pl.multiple_of(low, 16), ROWS)]
                wait = remote(dst, dst, a_send.at[0, i], a_recv.at[there, i], me.sibling)
                if k == 0:

                    @pl.when(me.c != core)
                    def _():
                        wait.wait_recv()
                else:
                    wait.wait_recv()
    stage_a[-2].wait()
    stage_a[-1].wait()
    for k in (2, 1, 3):
        ref = kv.at[me.z, me.line]
        copy = remote(ref, ref, b_send.at[k - 1], b_recv.at[k - 1], me.line_peer(k))
        copy.start()
        sent.append(copy)
    spread(me.line, 0)
    for n in range(2, 8):
        pack_and_send(n)
    for k in (1, 3, 2):
        piece = (me.line + k) % SIDE
        ref = kv.at[me.z, piece]
        remote(ref, ref, b_send.at[0], b_recv.at[SIDE - k - 1], me.sibling).wait_recv()
        spread(piece, SIDE - k)
    for k in (1, 3, 2):
        for index in range(SIDE):
            ref = kv.at[(me.z + k) % SIDE, (me.line + SIDE - index) % SIDE]
            remote(ref, ref, c_send.at[0, 0], c_recv.at[index, SIDE - k - 1], me.sibling).wait_recv()
    for k in range(SIDE):
        for core in (0, 1):
            there, device = me.source(k, core)

            def arrived(there=there):
                remote(recv.at[there], recv.at[there], x_send.at[0], x_recv.at[there], me.sibling).wait_recv()
                remote(slots.at[there], slots.at[there], sl_send.at[0], sl_recv.at[there], me.sibling).wait_recv()

            if k == 0:
                pl.when(me.c != core)(arrived)
            else:
                arrived()
    for copy in stage_a[:-2] + sent:
        if isinstance_remote(copy):
            copy.wait_send()
        else:
            copy.wait()


def isinstance_remote(copy):
    return copy.is_remote if hasattr(copy, "is_remote") else copy.device_id is not None


def attention_kernel(recv, slots, kv, ret, dkv, xu, ou):
    c = lax.axis_index("resp") % 2

    def one_hot(i):
        slot = slots[i][0:1, :LIVE].astype(jnp.int32)
        return jnp.where(lax.broadcasted_iota(jnp.int32, (TOKENS, LIVE), 0) == slot, 1.0, 0.0).astype(BF16)

    def unpack(i, carry):
        rows = dot(one_hot(i), recv[i], NN).astype(BF16)
        xu[:, pl.ds(pl.multiple_of(i * SLOTS, SLOTS), SLOTS), :] = rows.reshape(RESPONSES, SLOTS, MSG)
        return carry

    lax.fori_loop(0, 8, unpack, 0)

    own_rows = lax.broadcasted_iota(jnp.int32, (WIDTH, WIDTH), 0)
    own_cols = lax.broadcasted_iota(jnp.int32, (WIDTH, WIDTH), 1)
    own_mask = (own_rows >> 4 == own_cols >> 4) & (own_cols <= own_rows)
    own_mask = jnp.concatenate([own_mask] * GROUP, axis=0)

    def prompt(g, carry):
        gy, gz = g // SIDE, g % SIDE

        def chunk(i, quarter):
            piece = gy * (1 - c) + quarter * c
            low = (i * PREFIX + quarter * 96) * (1 - c) + (gy * 2 + i) * 96 * c
            return gz, piece, pl.ds(pl.multiple_of(low, 16), 96)

        def heads(low):
            return jnp.concatenate([xu[g, :, low + a * WIDTH : low + (a + 1) * WIDTH] for a in range(GROUP)], axis=0)

        queries, grads = heads(0), heads(GW)
        keys = jnp.concatenate([kv[chunk(0, i)] for i in range(SIDE)] + [xu[g, :, 2 * GW : 2 * GW + WIDTH]], axis=0)
        values = jnp.concatenate([kv[chunk(1, i)] for i in range(SIDE)] + [xu[g, :, 2 * GW + WIDTH :]], axis=0)
        scores = dot(queries, keys, NT)
        scores = jnp.concatenate(
            [scores[:, :PREFIX], jnp.where(own_mask, scores[:, PREFIX:], -1e30)], axis=1
        )
        top = jnp.max(scores, axis=1, keepdims=True)
        weights = jnp.exp2((scores - top) * EXP2_SCALE)
        total = jnp.sum(weights, axis=1, keepdims=True)
        over = 1.0 / total
        half = weights.astype(BF16)
        out = dot(half, values, NN) * over
        scaled = (grads.astype(F32) * over).astype(BF16)
        row_dot = jnp.sum(scaled.astype(F32) * out, axis=1, keepdims=True)
        score_grad = (weights * (dot(scaled, values, NT) - row_dot)).astype(BF16)
        query_grad = dot(score_grad, keys, NN) * SCALE
        key_grad = (dot(score_grad, queries, TN) * SCALE).astype(BF16)
        value_grad = dot(half, scaled, TN).astype(BF16)
        for i, rows in enumerate((key_grad, value_grad)):
            for quarter in range(SIDE):
                dkv[chunk(i, quarter)] = rows[quarter * 96 : (quarter + 1) * 96]
        for a in range(GROUP):
            ou[g, :, a * WIDTH : (a + 1) * WIDTH] = out[a * WIDTH : (a + 1) * WIDTH].astype(BF16)
            ou[g, :, GW + a * WIDTH : GW + (a + 1) * WIDTH] = query_grad[a * WIDTH : (a + 1) * WIDTH].astype(BF16)
        ou[g, :, 2 * GW : 2 * GW + WIDTH] = key_grad[PREFIX:]
        ou[g, :, 2 * GW + WIDTH :] = value_grad[PREFIX:]
        return carry

    lax.fori_loop(0, RESPONSES, prompt, 0)

    def repack(i, carry):
        rows = ou[:, pl.ds(pl.multiple_of(i * SLOTS, SLOTS), SLOTS), :].reshape(TOKENS, MSG)
        ret[i] = dot(one_hot(i), rows, TN).astype(BF16)
        return carry

    lax.fori_loop(0, 8, repack, 0)


def return_kernel(
    ret, dkv, back, grads,
    own, got_c, sum_c, got_b, final, in_sem, r_send, r_recv, c_send, c_recv, b_send, b_recv, a_send, a_recv, own_sem,
):
    me = Place()
    load = pltpu.make_async_copy(dkv.at[me.z], own, in_sem)
    load.start()
    me.barrier()
    sent = []
    for step, offset in enumerate((0, 1, 3, 2)):
        piece = (me.line + offset) % SIDE
        for k in (2, 1, 3):
            copy = remote(dkv.at[(me.z + k) % SIDE, piece], got_c.at[k - 1, piece], c_send.at[step, k - 1], c_recv.at[step, k - 1], me.z_peer(k))
            copy.start()
            sent.append(copy)
    local = []
    for k in (2, 1, 3, 0):
        for core in (0, 1):
            there, device = me.source(k, core)
            index = 2 * k + core
            if k == 0:

                @pl.when(me.c == core)
                def _():
                    pltpu.make_async_copy(ret.at[there], back.at[me.head], own_sem.at[0]).start()

                @pl.when(me.c != core)
                def _():
                    remote(ret.at[there], back.at[me.head], r_send.at[index], r_recv.at[me.head], device).start()
            else:
                copy = remote(ret.at[there], back.at[me.head], r_send.at[index], r_recv.at[me.head], device)
                copy.start()
                sent.append(copy)
    load.wait()
    for step, offset in enumerate((0, 1, 3, 2)):
        piece = (me.line + offset) % SIDE
        for k in (1, 3, 2):
            ref = got_c.at[k - 1, piece]
            remote(ref, ref, c_send.at[0, 0], c_recv.at[step, k - 1], me.sibling).wait_recv()
        total = own[piece].astype(F32) + got_c[0, piece].astype(F32) + got_c[1, piece].astype(F32) + got_c[2, piece].astype(F32)
        if offset == 0:
            final[...] = total
        else:
            sum_c[offset - 1] = total.astype(BF16)
            copy = remote(sum_c.at[offset - 1], got_b.at[offset - 1], b_send.at[offset - 1], b_recv.at[offset - 1], me.line_peer(offset))
            copy.start()
            sent.append(copy)
    for k in (1, 3, 2):
        ref = got_b.at[k - 1]
        remote(ref, ref, b_send.at[0], b_recv.at[k - 1], me.sibling).wait_recv()
    total = final[...] + got_b[0].astype(F32) + got_b[1].astype(F32) + got_b[2].astype(F32)
    sum_c[3] = total.astype(BF16)
    for k in (2, 1, 3, 0):
        for core in (0, 1):
            there, device = me.source(k, core)
            index = 2 * k + core
            sx = (me.x + k) % SIDE * (1 - me.c) + me.x * me.c
            sy = me.y * (1 - me.c) + (me.y + k) % SIDE * me.c
            for i in (0, 1):
                low = (i * PREFIX + (2 * sx + core) * ROWS) * (1 - me.c) + ((sy * 2 + i) * 2 * ROWS + core * ROWS) * me.c
                src = sum_c.at[3, pl.ds(pl.multiple_of(low, 16), ROWS)]
                dst = grads.at[me.head, i]
                if k == 0:

                    @pl.when(me.c == core)
                    def _():
                        pltpu.make_async_copy(src, dst, own_sem.at[1 + i]).start()

                    @pl.when(me.c != core)
                    def _():
                        remote(src, dst, a_send.at[index, i], a_recv.at[me.head, i], device).start()
                else:
                    copy = remote(src, dst, a_send.at[index, i], a_recv.at[me.head, i], device)
                    copy.start()
                    sent.append(copy)
    for head, _, device in me.routes:
        if device is None:
            pltpu.make_async_copy(back.at[head], back.at[head], own_sem.at[0]).wait()
            for i in (0, 1):
                pltpu.make_async_copy(grads.at[head, i], grads.at[head, i], own_sem.at[1 + i]).wait()
        else:
            remote(back.at[head], back.at[head], r_send.at[0], r_recv.at[head], me.sibling).wait_recv()
            for i in (0, 1):
                remote(grads.at[head, i], grads.at[head, i], a_send.at[0, i], a_recv.at[head, i], me.sibling).wait_recv()
    for copy in sent:
        copy.wait_send()
    for core in (0, 1):

        @pl.when(me.c != core)
        def _():
            there, device = me.source(0, core)
            remote(ret.at[there], back.at[me.head], r_send.at[core], r_recv.at[me.head], device).wait_send()
            for i in (0, 1):
                ref = sum_c.at[3, pl.ds(0, ROWS)]
                remote(ref, grads.at[me.head, i], a_send.at[core, i], a_recv.at[me.head, i], device).wait_send()


def unpack_kernel(len_ref, prm_ref, back, grads, attn, query, key, value, prefix_key, prefix_value, pack):
    @pl.when(pl.program_id(0) == 0)
    def _():
        row, _ = pack_rows(len_ref, prm_ref)
        pack[...] = one_hot_pack(row)

    rows = dot(pack[...], back[0], TN).astype(BF16)
    attn[...] = rows[:, :GW]
    query[...] = rows[:, GW : 2 * GW]
    key[...] = rows[:, 2 * GW : 2 * GW + WIDTH]
    value[...] = rows[:, 2 * GW + WIDTH :]
    prefix_key[...] = grads[0, 0].astype(F32)
    prefix_value[...] = grads[0, 1].astype(F32)


def spec(space):
    return pl.BlockSpec(memory_space=space)


DMA = pltpu.SemaphoreType.DMA


def local(queries, grad_out, response_keys, response_values, prompt_prefix_keys, prompt_prefix_values, lengths, prompt_of):
    q, g = queries.reshape(TOKENS, KEY_HEADS * GW), grad_out.reshape(TOKENS, KEY_HEADS * GW)
    k, v = response_keys.reshape(TOKENS, KEY_HEADS * WIDTH), response_values.reshape(TOKENS, KEY_HEADS * WIDTH)
    pk, pv = prompt_prefix_keys.reshape(ROWS, KEY_HEADS * WIDTH), prompt_prefix_values.reshape(ROWS, KEY_HEADS * WIDTH)
    lens, prompts = lengths.reshape(RESPONSES), prompt_of.reshape(RESPONSES)
    recv, slots, kv = pl.pallas_call(
        scatter_kernel,
        out_shape=(
            jax.ShapeDtypeStruct((8, LIVE, MSG), BF16),
            jax.ShapeDtypeStruct((8, 8, LIVE), F32),
            jax.ShapeDtypeStruct((SIDE, SIDE, PIECE, WIDTH), BF16),
        ),
        in_specs=[spec(pltpu.SMEM)] * 2 + [spec(pl.ANY)] * 6,
        out_specs=(spec(pl.ANY),) * 3,
        scratch_shapes=[
            pltpu.VMEM((8, TOKENS, MSG), BF16),
            pltpu.VMEM((8, LIVE, MSG), BF16),
            pltpu.VMEM((8, LIVE), F32),
            DMA((8,)), DMA((8,)), DMA((8,)), DMA((8,)), DMA((8,)), DMA((8, 2)), DMA((8, 2)),
            DMA((3,)), DMA((3,)), DMA((4, 3)), DMA((4, 3)), DMA((4,)),
        ],
        compiler_params=pltpu.CompilerParams(collective_id=0, has_side_effects=True, vmem_limit_bytes=VMEM_LIMIT),
    )(lens, prompts, q, g, k, v, pk, pv)
    ret, dkv = pl.pallas_call(
        attention_kernel,
        out_shape=(
            jax.ShapeDtypeStruct((8, LIVE, MSG), BF16),
            jax.ShapeDtypeStruct((SIDE, SIDE, PIECE, WIDTH), BF16),
        ),
        in_specs=[spec(pltpu.VMEM)] * 3,
        out_specs=(spec(pltpu.VMEM),) * 2,
        scratch_shapes=[pltpu.VMEM((RESPONSES, 8 * SLOTS, MSG), BF16)] * 2,
        compiler_params=pltpu.CompilerParams(vmem_limit_bytes=VMEM_LIMIT),
    )(recv, slots, kv)
    back, grads = pl.pallas_call(
        return_kernel,
        out_shape=(
            jax.ShapeDtypeStruct((8, LIVE, MSG), BF16),
            jax.ShapeDtypeStruct((8, 2, ROWS, WIDTH), BF16),
        ),
        in_specs=[spec(pl.ANY)] * 2,
        out_specs=(spec(pl.ANY),) * 2,
        scratch_shapes=[
            pltpu.VMEM((SIDE, PIECE, WIDTH), BF16),
            pltpu.VMEM((3, SIDE, PIECE, WIDTH), BF16),
            pltpu.VMEM((SIDE, PIECE, WIDTH), BF16),
            pltpu.VMEM((3, PIECE, WIDTH), BF16),
            pltpu.VMEM((PIECE, WIDTH), F32),
            DMA, DMA((8,)), DMA((8,)), DMA((4, 3)), DMA((4, 3)), DMA((3,)), DMA((3,)), DMA((8, 2)), DMA((8, 2)), DMA((3,)),
        ],
        compiler_params=pltpu.CompilerParams(collective_id=1, has_side_effects=True, vmem_limit_bytes=VMEM_LIMIT),
    )(ret, dkv)
    wide = pl.BlockSpec((TOKENS, GW), lambda h, *_: (0, h))
    narrow = pl.BlockSpec((TOKENS, WIDTH), lambda h, *_: (0, h))
    prefix = pl.BlockSpec((ROWS, WIDTH), lambda h, *_: (0, h))
    outs = pl.pallas_call(
        unpack_kernel,
        grid_spec=pltpu.PrefetchScalarGridSpec(
            num_scalar_prefetch=2,
            grid=(KEY_HEADS,),
            in_specs=[
                pl.BlockSpec((1, LIVE, MSG), lambda h, *_: (h, 0, 0)),
                pl.BlockSpec((1, 2, ROWS, WIDTH), lambda h, *_: (h, 0, 0, 0)),
            ],
            out_specs=[wide, wide, narrow, narrow, prefix, prefix],
            scratch_shapes=[pltpu.VMEM((LIVE, TOKENS), BF16)],
        ),
        out_shape=[
            jax.ShapeDtypeStruct(q.shape, BF16),
            jax.ShapeDtypeStruct(q.shape, BF16),
            jax.ShapeDtypeStruct(k.shape, BF16),
            jax.ShapeDtypeStruct(k.shape, BF16),
            jax.ShapeDtypeStruct(pk.shape, F32),
            jax.ShapeDtypeStruct(pk.shape, F32),
        ],
        compiler_params=pltpu.CompilerParams(vmem_limit_bytes=VMEM_LIMIT),
    )(lens, prompts, back, grads)
    shapes = (queries, queries, response_keys, response_keys, prompt_prefix_keys, prompt_prefix_keys)
    return tuple(out.reshape(like.shape) for out, like in zip(outs, shapes))


def solution(mesh):
    five, three = P("prompt", "resp", None, None, None), P("prompt", "resp", None)
    return jax.shard_map(
        local,
        mesh=mesh,
        in_specs=(five, five, five, five, three, three, three, three),
        out_specs=(five, five, five, five, three, three),
        check_vma=False,
    )
```

profile of v0, /device:TPU:1, one launch (start us, length us, event | category | flops | bytes accessed | tf_op | source)
XLA Modules:
  0.0 152.8 jit_solution(5280604434098938977)
XLA Ops:
  0.6 59.4 %shard_map.127 = (bf16[8,160,1536]{2,1,0:T(8,128)(2,1)}, f32[8,8,160]{2,1,0:T(8,128)}, bf16[4,4,768,128]{3,2,1,0:T(8,128)(2,1)}) custom-call(s32[16]{0:T(128)} %bitcast.20, s32[16]{0:T(128)} %bitcast.22, bf16[256,5120]{1,0:T(8,128)(2,1)} %bitcast.14, bf16[256,5120]{1,0:T(8,128)(2,1)} %bitcast.15, bf16[256,1024]{1,0:T(8,128)(2,1)} %bitcast.16, ...), custom_call_target="tpu_custom_call" | custom-call | tf_op jit(solution)/shard_map/pallas_call | solution.py:423
  60.0 35.3 %shard_map.128 = (bf16[8,160,1536]{2,1,0:T(8,128)(2,1)}, bf16[4,4,768,128]{3,2,1,0:T(8,128)(2,1)}) custom-call(bf16[8,160,1536]{2,1,0:T(8,128)(2,1)} %get-tuple-element.19.recv, f32[8,8,160]{2,1,0:T(8,128)} %get-tuple-element.20.slots, bf16[4,4,768,128]{3,2,1,0:T(8,128)(2,1)} %get-tuple-element.21.kv), custom_call_target="tpu_custom_call" | custom-call | tf_op jit(solution)/shard_map/pallas_call | solution.py:441
  95.3 48.8 %shard_map.129 = (bf16[8,160,1536]{2,1,0:T(8,128)(2,1)}, bf16[8,2,48,128]{3,2,1,0:T(8,128)(2,1)}) custom-call(bf16[8,160,1536]{2,1,0:T(8,128)(2,1)} %get-tuple-element.22.ret, bf16[4,4,768,128]{3,2,1,0:T(8,128)(2,1)} %get-tuple-element.23.dkv), custom_call_target="tpu_custom_call" | custom-call | tf_op jit(solution)/shard_map/pallas_call | solution.py:452
  144.1 8.6 %shard_map.130 = (bf16[256,5120]{1,0:T(8,128)(2,1)}, bf16[256,5120]{1,0:T(8,128)(2,1)}, bf16[256,1024]{1,0:T(8,128)(2,1)}, bf16[256,1024]{1,0:T(8,128)(2,1)}, f32[48,1024]{1,0:T(8,128)}, /*index=5*/f32[48,1024]{1,0:T(8,128)}) custom-call(s32[16]{0:T(128)} %bitcast.21, s32[16]{0:T(128)} %bitcast.23, bf16[8,160,1536]{2,1,0:T(8,128)(2,1)} %get-tuple-element.24.back, ...), custom_call_target="tpu_custom_call" | custom-call | tf_op jit(solution)/shard_map/pallas_call | solution.py:473
where the time goes:
time: 153 us
  Pallas kernels  152 us (99%)
    pallas_call x1, Pallas kernels, local(): pl.pallas_call(scatter_kernel, out_shape=(jax.ShapeDtypeStruct((8, LIVE,...  59.4 us
    pallas_call x1, Pallas kernels, local(): pl.pallas_call(return_kernel, out_shape=(jax.ShapeDtypeStruct((8, LIVE, M...  48.8 us
    pallas_call x1, Pallas kernels, local(): pl.pallas_call(attention_kernel, out_shape=(jax.ShapeDtypeStruct((8, LIVE...  35.3 us
    pallas_call x1, Pallas kernels, local(): pl.pallas_call(unpack_kernel, grid_spec=pltpu.PrefetchScalarGridSpec(num_...  8.65 us

commit v1 on v0

v1 whole, which is shorter than its diff:
```python
import jax
import jax.numpy as jnp
from jax import lax
from jax.experimental import pallas as pl
from jax.experimental.pallas import tpu as pltpu
from jax.sharding import PartitionSpec as P

KEY_HEADS = 8
WIDTH = 128
GROUP = 5
SLOTS = 16
RESPONSES = 16
TOKENS = SLOTS * RESPONSES
LIVE = 160
PREFIX = 384
SIDE = 4
ROWS = PREFIX // 8
PIECE = 2 * PREFIX
GW = GROUP * WIDTH
MSG = 2 * GW + 2 * WIDTH
MESH = pl.DeviceIdType.MESH
BF16 = jnp.bfloat16
F32 = jnp.float32
SCALE = WIDTH**-0.5
EXP2_SCALE = SCALE * 1.4426950408889634
VMEM_LIMIT = 58 * 1024 * 1024


class Place:
    def __init__(self):
        prompt, resp = lax.axis_index("prompt"), lax.axis_index("resp")
        self.y, self.z = prompt // SIDE, prompt % SIDE
        self.x, self.c = resp // 2, resp % 2
        self.prompt, self.resp = prompt, resp
        x, y, z, c = self.x, self.y, self.z, self.c
        self.sibling = (prompt, x * 2 + 1 - c)
        self.home_slot = 2 * (x * (1 - c) + y * c) + c
        self.head = x * (1 - c) + (SIDE + y) * c
        self.line = y * (1 - c) + x * c
        self.routes = []
        for k in (2, 1, 3):
            xd, yd = (x + k) % SIDE, (y + k) % SIDE
            self.routes.append((xd, 2 * x + c, (prompt, 2 * xd)))
            self.routes.append((SIDE + yd, 2 * y + c, (yd * SIDE + z, 2 * x + 1)))
        self.routes.append(((SIDE + y) * (1 - c) + x * c, 2 * y * (1 - c) + (2 * x + 1) * c, self.sibling))
        self.routes.append((self.head, self.home_slot, None))

    def source(self, k, core):
        along = (self.x * (1 - self.c) + self.y * self.c + k) % SIDE
        prompt = self.prompt * (1 - self.c) + (along * SIDE + self.z) * self.c
        resp = (along * 2 + core) * (1 - self.c) + (2 * self.x + core) * self.c
        return 2 * along + core, (prompt, resp)

    def line_peer(self, k):
        prompt = ((self.y + k * (1 - self.c)) % SIDE) * SIDE + self.z
        return (prompt, ((self.x + k * self.c) % SIDE) * 2 + self.c)

    def z_peer(self, k):
        return (self.y * SIDE + (self.z + k) % SIDE, self.resp)

    def barrier(self):
        sem = pltpu.get_barrier_semaphore()
        peers = [self.sibling]
        for k in (1, 2, 3):
            peers.append(self.z_peer(k))
            for core in (0, 1):
                peers.append((self.prompt, ((self.x + k) % SIDE) * 2 + core))
                peers.append((((self.y + k) % SIDE) * SIDE + self.z, 2 * self.x + core))
        for peer in peers:
            pl.semaphore_signal(sem, inc=1, device_id=peer, device_id_type=MESH)
        pl.semaphore_wait(sem, len(peers))


def remote(src, dst, send, recv, device):
    return pltpu.make_async_remote_copy(
        src_ref=src, dst_ref=dst, send_sem=send, recv_sem=recv, device_id=device, device_id_type=MESH
    )


def pack_rows(len_ref, prm_ref):
    lane = lax.broadcasted_iota(jnp.int32, (1, TOKENS), 1)
    response, token = lane >> 4, lane & (SLOTS - 1)
    row = jnp.full((1, TOKENS), -1, jnp.int32)
    slot = jnp.zeros((1, TOKENS), jnp.int32)
    start = jnp.int32(0)
    for j in range(RESPONSES):
        length = len_ref[j]
        mine = response == j
        row = jnp.where(mine & (token < length), start + token, row)
        slot = jnp.where(mine, prm_ref[j] * SLOTS + token, slot)
        start = start + length
    return row, slot


def one_hot_pack(row):
    packed = lax.broadcasted_iota(jnp.int32, (LIVE, TOKENS), 0)
    return jnp.where(packed == row, 1.0, 0.0).astype(BF16)


def dot(a, b, dims):
    return lax.dot_general(a, b, (dims, ((), ())), preferred_element_type=F32)


NN = ((1,), (0,))
NT = ((1,), (1,))
TN = ((0,), (0,))


def main_kernel(
    len_ref, prm_ref, q, g, k, v, pk, pv, back, grads,
    xb, send, slot_send, recv, slots, kv, xu, ou, dkv, half_sum, got_m, got_p, line_sum, got_b, final,
    in_sem, x_send, x_recv, sl_send, sl_recv, a_send, a_recv, b_send, b_recv,
    cp_send, cp_recv, cm_send, cm_recv, f_send, f_recv,
    h_send, h_recv, gm_send, gm_recv, gp_send, gp_recv, d_send, d_recv, e_send, e_recv, r_send, r_recv, own_sem,
):
    me = Place()
    routes = me.routes
    after, before = me.z_peer(1), me.z_peer(SIDE - 1)
    plane_of = lambda k: (me.z + k) % SIDE
    piece_of = lambda offset: (me.line + offset) % SIDE

    def await_recv(ref, sem):
        remote(ref, ref, x_send.at[0], sem, me.sibling).wait_recv()

    def await_send(ref, sem):
        remote(ref, ref, sem, x_recv.at[0], me.sibling).wait_send()

    for n, (head, _, _) in enumerate(routes):
        wide = pl.ds(pl.multiple_of(head * GW, WIDTH), GW)
        narrow = pl.ds(pl.multiple_of(head * WIDTH, WIDTH), WIDTH)
        for src, cols, low, size in ((q, wide, 0, GW), (g, wide, GW, GW), (k, narrow, 2 * GW, WIDTH), (v, narrow, 2 * GW + WIDTH, WIDTH)):
            pltpu.make_async_copy(src.at[:, cols], xb.at[n, :, pl.ds(low, size)], in_sem.at[n]).start()
    me.barrier()

    for n, (head, there, device) in enumerate(routes):
        narrow = pl.ds(pl.multiple_of(head * WIDTH, WIDTH), WIDTH)
        on_y = head // SIDE
        for i, src in enumerate((pk, pv)):
            piece = me.y * (1 - on_y) + me.x * on_y
            low = (i * PREFIX + me.resp * ROWS) * (1 - on_y) + ((me.y * 2 + i) * 2 * ROWS + me.c * ROWS) * on_y
            dst = kv.at[me.z, piece, pl.ds(pl.multiple_of(low, 16), ROWS)]
            if device is None:
                pltpu.make_async_copy(src.at[:, narrow], dst, own_sem.at[1 + i]).start()
            else:
                remote(src.at[:, narrow], dst, a_send.at[n, i], a_recv.at[there, i], device).start()

    row, slot = pack_rows(len_ref, prm_ref)
    pack = one_hot_pack(row)
    slot8 = jnp.broadcast_to(slot, (8, TOKENS)).astype(F32).astype(BF16)
    slot_send[...] = dot(slot8, pack, NT)
    for n, (_, there, device) in enumerate(routes):
        if device is None:
            pltpu.make_async_copy(slot_send, slots.at[there], own_sem.at[3]).start()
        else:
            remote(slot_send, slots.at[there], sl_send.at[n], sl_recv.at[there], device).start()

    def pack_and_send(n):
        _, there, device = routes[n]
        pltpu.make_async_copy(xb.at[n], xb.at[n], in_sem.at[n]).wait()
        rows = dot(pack, xb[n], NN).astype(BF16)
        if device is None:
            recv[there] = rows
        else:
            send[n] = rows
            remote(send.at[n], recv.at[there], x_send.at[n], x_recv.at[there], device).start()

    def spread(offset):
        ref = kv.at[me.z, piece_of(offset)]
        remote(ref, ref, cp_send.at[offset], cp_recv.at[offset], after).start()
        remote(ref, ref, cm_send.at[offset], cm_recv.at[offset], before).start()

    def line_rows(k, core, i):
        sx = (me.x + k) % SIDE * (1 - me.c) + me.x * me.c
        sy = me.y * (1 - me.c) + (me.y + k) % SIDE * me.c
        low = (i * PREFIX + (2 * sx + core) * ROWS) * (1 - me.c) + ((sy * 2 + i) * 2 * ROWS + core * ROWS) * me.c
        return pl.ds(pl.multiple_of(low, 16), ROWS)

    pack_and_send(0)
    pack_and_send(1)
    for i in (0, 1):
        dst = kv.at[me.z, me.line, line_rows(0, 0, i)]
        pltpu.make_async_copy(dst, dst, own_sem.at[1 + i]).wait()
    for k in range(SIDE):
        for core in (0, 1):
            there, _ = me.source(k, core)
            for i in (0, 1):
                dst = kv.at[me.z, me.line, line_rows(k, core, i)]
                if k == 0:
                    pl.when(me.c != core)(lambda dst=dst, there=there, i=i: await_recv(dst, a_recv.at[there, i]))
                else:
                    await_recv(dst, a_recv.at[there, i])
    for k in (1, 3, 2):
        ref = kv.at[me.z, me.line]
        remote(ref, ref, b_send.at[k - 1], b_recv.at[k - 1], me.line_peer(k)).start()
    spread(0)
    pack_and_send(2)
    pack_and_send(3)
    for k in (1, 3, 2):
        await_recv(kv.at[me.z, piece_of(k)], b_recv.at[SIDE - k - 1])
        spread(k)
    for n in range(4, 8):
        pack_and_send(n)
    for offset in (0, 1):
        ref = kv.at[plane_of(3), piece_of(offset)]
        await_recv(ref, cp_recv.at[offset])
        remote(ref, ref, f_send.at[offset], f_recv.at[offset], after).start()
    for offset in (3, 2):
        ref = kv.at[plane_of(1), piece_of(offset)]
        await_recv(ref, cm_recv.at[offset])
        remote(ref, ref, f_send.at[offset], f_recv.at[offset], before).start()

    def one_hot(i):
        slot = slots[i][0:1].astype(jnp.int32)
        return jnp.where(lax.broadcasted_iota(jnp.int32, (TOKENS, LIVE), 0) == slot, 1.0, 0.0).astype(BF16)

    pltpu.make_async_copy(slot_send, slots.at[me.home_slot], own_sem.at[3]).wait()

    def unpack(m, carry):
        there = (me.home_slot + m) % 8

        @pl.when(m > 0)
        def _():
            await_recv(slots.at[there], sl_recv.at[there])
            await_recv(recv.at[there], x_recv.at[there])

        rows = dot(one_hot(there), recv[there], NN).astype(BF16)
        xu[:, pl.ds(pl.multiple_of(there * SLOTS, SLOTS), SLOTS), :] = rows.reshape(RESPONSES, SLOTS, MSG)
        return carry

    lax.fori_loop(0, 8, unpack, 0)
    for offset in (0, 1):
        await_recv(kv.at[plane_of(1), piece_of(offset)], cm_recv.at[offset])
    for offset in (3, 2):
        await_recv(kv.at[plane_of(3), piece_of(offset)], cp_recv.at[offset])
    for offset in (0, 1, 3, 2):
        await_recv(kv.at[plane_of(2), piece_of(offset)], f_recv.at[offset])

    own_rows = lax.broadcasted_iota(jnp.int32, (WIDTH, WIDTH), 0)
    own_cols = lax.broadcasted_iota(jnp.int32, (WIDTH, WIDTH), 1)
    own_mask = (own_rows >> 4 == own_cols >> 4) & (own_cols <= own_rows)
    own_mask = jnp.concatenate([own_mask] * GROUP, axis=0)
    c = me.c

    def prompt(gz, gy):
        number = gy * SIDE + gz

        def chunk(i, quarter):
            piece = gy * (1 - c) + quarter * c
            low = (i * PREFIX + quarter * 96) * (1 - c) + (gy * 2 + i) * 96 * c
            return gz, piece, pl.ds(pl.multiple_of(low, 16), 96)

        def heads(low):
            return jnp.concatenate([xu[number, :, low + a * WIDTH : low + (a + 1) * WIDTH] for a in range(GROUP)], axis=0)

        def put(low, rows):
            ou[:, gz, pl.ds(pl.multiple_of(gy * SLOTS, SLOTS), SLOTS), low : low + WIDTH] = rows.reshape(8, SLOTS, WIDTH)

        queries, grad_rows = heads(0), heads(GW)
        keys = jnp.concatenate([kv[chunk(0, i)] for i in range(SIDE)] + [xu[number, :, 2 * GW : 2 * GW + WIDTH]], axis=0)
        values = jnp.concatenate([kv[chunk(1, i)] for i in range(SIDE)] + [xu[number, :, 2 * GW + WIDTH :]], axis=0)
        scores = dot(queries, keys, NT)
        scores = jnp.concatenate([scores[:, :PREFIX], jnp.where(own_mask, scores[:, PREFIX:], -1e30)], axis=1)
        top = jnp.max(scores, axis=1, keepdims=True)
        weights = jnp.exp2((scores - top) * EXP2_SCALE)
        over = 1.0 / jnp.sum(weights, axis=1, keepdims=True)
        half = weights.astype(BF16)
        out = dot(half, values, NN) * over
        scaled = (grad_rows.astype(F32) * over).astype(BF16)
        row_dot = jnp.sum(scaled.astype(F32) * out, axis=1, keepdims=True)
        score_grad = (weights * (dot(scaled, values, NT) - row_dot)).astype(BF16)
        query_grad = dot(score_grad, keys, NN) * SCALE
        key_grad = (dot(score_grad, queries, TN) * SCALE).astype(BF16)
        value_grad = dot(half, scaled, TN).astype(BF16)
        for i, rows in enumerate((key_grad, value_grad)):
            for quarter in range(SIDE):
                dkv[chunk(i, quarter)] = rows[quarter * 96 : (quarter + 1) * 96]
        for a in range(GROUP):
            put(a * WIDTH, out[a * WIDTH : (a + 1) * WIDTH].astype(BF16))
            put(GW + a * WIDTH, query_grad[a * WIDTH : (a + 1) * WIDTH].astype(BF16))
        put(2 * GW, key_grad[PREFIX:])
        put(2 * GW + WIDTH, value_grad[PREFIX:])

    def to_after(offset):
        remote(dkv.at[plane_of(1), piece_of(offset)], got_m.at[offset], gm_send.at[offset], gm_recv.at[offset], after).start()

    def to_before(offset):
        remote(dkv.at[plane_of(3), piece_of(offset)], got_p.at[offset], gp_send.at[offset], gp_recv.at[offset], before).start()

    def plane(s, carry):
        gz = (me.z + 6 - s - s // 2 + 2 * (s // 3)) % SIDE

        def step(gy, inner):
            prompt(gz, gy)
            return inner

        lax.fori_loop(0, SIDE, step, 0)

        @pl.when(s == 0)
        def _():
            for offset in range(SIDE):
                device = after if offset < 2 else before
                remote(dkv.at[plane_of(2), piece_of(offset)], half_sum.at[offset], h_send.at[offset], h_recv.at[offset], device).start()

        @pl.when(s == 1)
        def _():
            to_after(2)
            to_after(3)

        @pl.when(s == 2)
        def _():
            to_before(0)
            to_before(1)
            for offset in range(SIDE):
                there = plane_of(1) if offset < 2 else plane_of(3)
                await_recv(half_sum.at[offset], h_recv.at[offset])
                total = dkv[there, piece_of(offset)].astype(F32) + half_sum[offset].astype(F32)
                dkv[there, piece_of(offset)] = total.astype(BF16)
                if offset < 2:
                    to_after(offset)
                else:
                    to_before(offset)

        for k in (2, 1, 3, 0):
            for core in (0, 1):
                there, device = me.source(k, core)
                index = 2 * k + core
                src, dst = ou.at[there, gz], back.at[me.head, gz]
                away = lambda: remote(src, dst, r_send.at[index], r_recv.at[me.head], device).start()
                if k == 0:
                    pl.when(c == core)(lambda: pltpu.make_async_copy(src, dst, own_sem.at[0]).start())
                    pl.when(c != core)(away)
                else:
                    away()
        return carry

    lax.fori_loop(0, SIDE, plane, 0)

    for offset in (1, 3, 2, 0):
        await_recv(got_m.at[offset], gm_recv.at[offset])
        await_recv(got_p.at[offset], gp_recv.at[offset])
        total = dkv[me.z, piece_of(offset)].astype(F32) + got_m[offset].astype(F32) + got_p[offset].astype(F32)
        if offset == 0:
            final[...] = total
        else:
            line_sum[offset - 1] = total.astype(BF16)
            remote(line_sum.at[offset - 1], got_b.at[offset - 1], d_send.at[offset - 1], d_recv.at[offset - 1], me.line_peer(offset)).start()
    for k in (1, 3, 2):
        await_recv(got_b.at[k - 1], d_recv.at[k - 1])
    line_sum[3] = (final[...] + got_b[0].astype(F32) + got_b[1].astype(F32) + got_b[2].astype(F32)).astype(BF16)
    for k in (2, 1, 3, 0):
        for core in (0, 1):
            _, device = me.source(k, core)
            index = 2 * k + core
            for i in (0, 1):
                src, dst = line_sum.at[3, line_rows(k, core, i)], grads.at[me.head, i]
                away = lambda: remote(src, dst, e_send.at[index, i], e_recv.at[me.head, i], device).start()
                if k == 0:
                    pl.when(c == core)(lambda: pltpu.make_async_copy(src, dst, own_sem.at[1 + i]).start())
                    pl.when(c != core)(away)
                else:
                    away()

    for head, _, device in routes:
        if device is None:
            pltpu.make_async_copy(back.at[head], back.at[head], own_sem.at[0]).wait()
            for i in (0, 1):
                pltpu.make_async_copy(grads.at[head, i], grads.at[head, i], own_sem.at[1 + i]).wait()
        else:
            await_recv(back.at[head], r_recv.at[head])
            for i in (0, 1):
                await_recv(grads.at[head, i], e_recv.at[head, i])
    for n in range(7):
        await_send(send.at[n], x_send.at[n])
        await_send(slot_send, sl_send.at[n])
        for i in (0, 1):
            await_send(grads.at[0, i], a_send.at[n, i])
    for k in range(3):
        await_send(line_sum.at[k], b_send.at[k])
        await_send(line_sum.at[k], d_send.at[k])
    for offset in range(SIDE):
        for sem in (cp_send, cm_send, f_send, h_send, gm_send, gp_send):
            await_send(got_m.at[offset], sem.at[offset])

    def sent_back(index):
        await_send(back.at[0], r_send.at[index])
        for i in (0, 1):
            await_send(grads.at[0, i], e_send.at[index, i])

    for index in range(8):
        if index < 2:
            pl.when(c != index)(lambda: sent_back(index))
        else:
            sent_back(index)


def unpack_kernel(len_ref, prm_ref, back, grads, attn, query, key, value, prefix_key, prefix_value, pick):
    @pl.when(pl.program_id(0) == 0)
    def _():
        lane = lax.broadcasted_iota(jnp.int32, (SLOTS, TOKENS), 1)
        token = lax.broadcasted_iota(jnp.int32, (SLOTS, TOKENS), 0)
        for j in range(RESPONSES):
            there = prm_ref[j]
            first = (there % SIDE) * SIDE * SLOTS + (there // SIDE) * SLOTS
            mine = (lane == first + token) & (token < len_ref[j])
            pick[j * SLOTS : (j + 1) * SLOTS, :] = jnp.where(mine, 1.0, 0.0).astype(BF16)

    rows = dot(pick[...], back[0].reshape(TOKENS, MSG), NN).astype(BF16)
    attn[...] = rows[:, :GW]
    query[...] = rows[:, GW : 2 * GW]
    key[...] = rows[:, 2 * GW : 2 * GW + WIDTH]
    value[...] = rows[:, 2 * GW + WIDTH :]
    prefix_key[...] = grads[0, 0].astype(F32)
    prefix_value[...] = grads[0, 1].astype(F32)


def spec(space):
    return pl.BlockSpec(memory_space=space)


DMA = pltpu.SemaphoreType.DMA


def local(queries, grad_out, response_keys, response_values, prompt_prefix_keys, prompt_prefix_values, lengths, prompt_of):
    q, g = queries.reshape(TOKENS, KEY_HEADS * GW), grad_out.reshape(TOKENS, KEY_HEADS * GW)
    k, v = response_keys.reshape(TOKENS, KEY_HEADS * WIDTH), response_values.reshape(TOKENS, KEY_HEADS * WIDTH)
    pk, pv = prompt_prefix_keys.reshape(ROWS, KEY_HEADS * WIDTH), prompt_prefix_values.reshape(ROWS, KEY_HEADS * WIDTH)
    lens, prompts = lengths.reshape(RESPONSES), prompt_of.reshape(RESPONSES)
    vmem = pltpu.VMEM
    back, grads = pl.pallas_call(
        main_kernel,
        out_shape=(
            jax.ShapeDtypeStruct((8, SIDE, SIDE * SLOTS, MSG), BF16),
            jax.ShapeDtypeStruct((8, 2, ROWS, WIDTH), BF16),
        ),
        in_specs=[spec(pltpu.SMEM)] * 2 + [spec(pl.ANY)] * 6,
        out_specs=(spec(pl.ANY),) * 2,
        scratch_shapes=[
            vmem((8, TOKENS, MSG), BF16), vmem((7, LIVE, MSG), BF16), vmem((8, LIVE), F32),
            vmem((8, LIVE, MSG), BF16), vmem((8, 8, LIVE), F32), vmem((SIDE, SIDE, PIECE, WIDTH), BF16),
            vmem((RESPONSES, 8 * SLOTS, MSG), BF16), vmem((8, SIDE, SIDE * SLOTS, MSG), BF16),
            vmem((SIDE, SIDE, PIECE, WIDTH), BF16), vmem((SIDE, PIECE, WIDTH), BF16), vmem((SIDE, PIECE, WIDTH), BF16),
            vmem((SIDE, PIECE, WIDTH), BF16), vmem((SIDE, PIECE, WIDTH), BF16), vmem((3, PIECE, WIDTH), BF16), vmem((PIECE, WIDTH), F32),
            DMA((8,)), DMA((8,)), DMA((8,)), DMA((8,)), DMA((8,)), DMA((8, 2)), DMA((8, 2)), DMA((3,)), DMA((3,)),
        ] + [DMA((SIDE,))] * 12 + [DMA((3,)), DMA((3,)), DMA((8, 2)), DMA((8, 2)), DMA((8,)), DMA((8,)), DMA((4,))],
        compiler_params=pltpu.CompilerParams(collective_id=0, has_side_effects=True, vmem_limit_bytes=VMEM_LIMIT),
    )(lens, prompts, q, g, k, v, pk, pv)
    wide = pl.BlockSpec((TOKENS, GW), lambda h, *_: (0, h))
    narrow = pl.BlockSpec((TOKENS, WIDTH), lambda h, *_: (0, h))
    prefix = pl.BlockSpec((ROWS, WIDTH), lambda h, *_: (0, h))
    outs = pl.pallas_call(
        unpack_kernel,
        grid_spec=pltpu.PrefetchScalarGridSpec(
            num_scalar_prefetch=2,
            grid=(KEY_HEADS,),
            in_specs=[
                pl.BlockSpec((1, SIDE, SIDE * SLOTS, MSG), lambda h, *_: (h, 0, 0, 0)),
                pl.BlockSpec((1, 2, ROWS, WIDTH), lambda h, *_: (h, 0, 0, 0)),
            ],
            out_specs=[wide, wide, narrow, narrow, prefix, prefix],
            scratch_shapes=[vmem((TOKENS, TOKENS), BF16)],
        ),
        out_shape=[
            jax.ShapeDtypeStruct(q.shape, BF16),
            jax.ShapeDtypeStruct(q.shape, BF16),
            jax.ShapeDtypeStruct(k.shape, BF16),
            jax.ShapeDtypeStruct(k.shape, BF16),
            jax.ShapeDtypeStruct(pk.shape, F32),
            jax.ShapeDtypeStruct(pk.shape, F32),
        ],
        compiler_params=pltpu.CompilerParams(vmem_limit_bytes=VMEM_LIMIT),
    )(lens, prompts, back, grads)
    shapes = (queries, queries, response_keys, response_keys, prompt_prefix_keys, prompt_prefix_keys)
    return tuple(out.reshape(like.shape) for out, like in zip(outs, shapes))


def solution(mesh):
    five, three = P("prompt", "resp", None, None, None), P("prompt", "resp", None)
    return jax.shard_map(
        local,
        mesh=mesh,
        in_specs=(five, five, five, five, three, three, three, three),
        out_specs=(five, five, five, five, three, three),
        check_vma=False,
    )
```

time: 153 us -> 110 us (0.72)
  Pallas kernels: 152 us -> 109 us
    pallas_call x3 -> x1, Pallas kernels: 143 us -> 99.6 us  [local(): pl.pallas_call(main_kernel, out_shape=(jax.ShapeDtypeStruct((8, SIDE, SID...]
where the time goes in v1:
time: 110 us
  Pallas kernels  109 us (99%)
    pallas_call x1, Pallas kernels, local(): pl.pallas_call(main_kernel, out_shape=(jax.ShapeDtypeStruct((8, SIDE, SID...  99.6 us
    pallas_call x1, Pallas kernels, local(): pl.pallas_call(unpack_kernel, grid_spec=pltpu.PrefetchScalarGridSpec(num_...  9.68 us

profile of v1, /device:TPU:1, one launch (start us, length us, event | category | flops | bytes accessed | tf_op | source)
XLA Modules:
  0.0 109.9 jit_solution(10880087650436794110)
XLA Ops:
  0.6 99.6 %shard_map.127 = (bf16[8,4,64,1536]{3,2,1,0:T(8,128)(2,1)}, bf16[8,2,48,128]{3,2,1,0:T(8,128)(2,1)}) custom-call(s32[16]{0:T(128)} %bitcast.20, s32[16]{0:T(128)} %bitcast.22, bf16[256,5120]{1,0:T(8,128)(2,1)} %bitcast.14, bf16[256,5120]{1,0:T(8,128)(2,1)} %bitcast.15, bf16[256,1024]{1,0:T(8,128)(2,1)} %bitcast.16, bf16[256,1024]{1,0:T(8,128)(2,1)} %bitcast.17, ...), custom_call_target="tpu_custom_call" | custom-call | tf_op jit(solution)/shard_map/pallas_call | solution.py:429
  100.3 9.7 %shard_map.128 = (bf16[256,5120]{1,0:T(8,128)(2,1)}, bf16[256,5120]{1,0:T(8,128)(2,1)}, bf16[256,1024]{1,0:T(8,128)(2,1)}, bf16[256,1024]{1,0:T(8,128)(2,1)}, f32[48,1024]{1,0:T(8,128)}, /*index=5*/f32[48,1024]{1,0:T(8,128)}) custom-call(s32[16]{0:T(128)} %bitcast.21, s32[16]{0:T(128)} %bitcast.23, bf16[8,4,64,1536]{3,2,1,0:T(8,128)(2,1)} %get-tuple-element.14.back, ...), custom_call_target="tpu_custom_call" | custom-call | tf_op jit(solution)/shard_map/pallas_call | solution.py:450

commit v2 on v1

v2 whole, which is shorter than its diff:
```python
import jax
import jax.numpy as jnp
from jax import lax
from jax.experimental import pallas as pl
from jax.experimental.pallas import tpu as pltpu
from jax.sharding import PartitionSpec as P

KEY_HEADS = 8
WIDTH = 128
GROUP = 5
SLOTS = 16
RESPONSES = 16
TOKENS = SLOTS * RESPONSES
LIVE = 160
PREFIX = 384
SIDE = 4
ROWS = PREFIX // 8
GW = GROUP * WIDTH
MSG = 2 * GW + 2 * WIDTH
MESH = pl.DeviceIdType.MESH
BF16 = jnp.bfloat16
F32 = jnp.float32
SCALE = WIDTH**-0.5
EXP2_SCALE = SCALE * 1.4426950408889634
BATCH = 4
HOLD = 14
EARLY = 0
SHIFT = 0
VMEM_LIMIT = 58 * 1024 * 1024


class Place:
    def __init__(self):
        prompt, resp = lax.axis_index("prompt"), lax.axis_index("resp")
        self.y, self.z = prompt // SIDE, prompt % SIDE
        self.x, self.c = resp // 2, resp % 2
        self.prompt, self.resp = prompt, resp
        x, y, z, c = self.x, self.y, self.z, self.c
        self.sibling = (prompt, x * 2 + 1 - c)
        self.home_slot = 2 * (x * (1 - c) + y * c) + c
        self.head = x * (1 - c) + (SIDE + y) * c
        self.line = y * (1 - c) + x * c
        self.routes = []
        for k in (2, 1, 3):
            xd, yd = (x + k) % SIDE, (y + k) % SIDE
            self.routes.append((xd, 2 * x + c, (prompt, 2 * xd)))
            self.routes.append((SIDE + yd, 2 * y + c, (yd * SIDE + z, 2 * x + 1)))
        self.routes.append(((SIDE + y) * (1 - c) + x * c, 2 * y * (1 - c) + (2 * x + 1) * c, self.sibling))
        self.routes.append((self.head, self.home_slot, None))

    def source(self, k, core):
        along = (self.x * (1 - self.c) + self.y * self.c + k) % SIDE
        prompt = self.prompt * (1 - self.c) + (along * SIDE + self.z) * self.c
        resp = (along * 2 + core) * (1 - self.c) + (2 * self.x + core) * self.c
        return 2 * along + core, (prompt, resp)

    def line_peer(self, k):
        prompt = ((self.y + k * (1 - self.c)) % SIDE) * SIDE + self.z
        return (prompt, ((self.x + k * self.c) % SIDE) * 2 + self.c)

    def z_peer(self, k):
        return (self.y * SIDE + (self.z + k) % SIDE, self.resp)

    def barrier(self):
        sem = pltpu.get_barrier_semaphore()
        peers = [self.sibling]
        for k in (1, 2, 3):
            peers.append(self.z_peer(k))
            for core in (0, 1):
                peers.append((self.prompt, ((self.x + k) % SIDE) * 2 + core))
                peers.append((((self.y + k) % SIDE) * SIDE + self.z, 2 * self.x + core))
        for peer in peers:
            pl.semaphore_signal(sem, inc=1, device_id=peer, device_id_type=MESH)
        pl.semaphore_wait(sem, len(peers))


def remote(src, dst, send, recv, device):
    return pltpu.make_async_remote_copy(
        src_ref=src, dst_ref=dst, send_sem=send, recv_sem=recv, device_id=device, device_id_type=MESH
    )


def pack_rows(len_ref, prm_ref):
    lane = lax.broadcasted_iota(jnp.int32, (1, TOKENS), 1)
    response, token = lane >> 4, lane & (SLOTS - 1)
    row = jnp.full((1, TOKENS), -1, jnp.int32)
    slot = jnp.zeros((1, TOKENS), jnp.int32)
    start = jnp.int32(0)
    for j in range(RESPONSES):
        length = len_ref[j]
        mine = response == j
        row = jnp.where(mine & (token < length), start + token, row)
        slot = jnp.where(mine, prm_ref[j] * SLOTS + token, slot)
        start = start + length
    return row, slot


def one_hot_pack(row):
    packed = lax.broadcasted_iota(jnp.int32, (LIVE, TOKENS), 0)
    return jnp.where(packed == row, 1.0, 0.0).astype(BF16)


def dot(a, b, dims):
    return lax.dot_general(a, b, (dims, ((), ())), preferred_element_type=F32)


NN = ((1,), (0,))
NT = ((1,), (1,))
TN = ((0,), (0,))


def main_kernel(
    len_ref, prm_ref, q, g, k, v, pk, pv, back, grads,
    xb, send, slot_send, recv, slots, kv, pkv, xu, ou, dkv, half_sum, got_m, got_p, plane_sum, got_y, got_x, final_y, final_x,
    in_sem, x_send, x_recv, sl_send, sl_recv, a_send, a_recv, b_send, b_recv,
    cp_send, cp_recv, cm_send, cm_recv, f_send, f_recv,
    h_send, h_recv, gm_send, gm_recv, gp_send, gp_recv, d_send, d_recv, e_send, e_recv, r_send, r_recv, own_sem,
):
    me = Place()
    routes = me.routes
    after, before = me.z_peer(1), me.z_peer(SIDE - 1)
    plane_of = lambda k: (me.z + k) % SIDE
    piece_of = lambda offset: (me.line + offset) % SIDE

    def core_rows(core):
        return pl.ds(pl.multiple_of(core * ROWS, 16), ROWS)

    def await_recv(ref, sem):
        remote(ref, ref, x_send.at[0], sem, me.sibling).wait_recv()

    def await_send(ref, sem):
        remote(ref, ref, sem, x_recv.at[0], me.sibling).wait_send()

    for n, (head, _, _) in enumerate(routes):
        wide = pl.ds(pl.multiple_of(head * GW, WIDTH), GW)
        narrow = pl.ds(pl.multiple_of(head * WIDTH, WIDTH), WIDTH)
        for src, cols, low, size in ((q, wide, 0, GW), (g, wide, GW, GW), (k, narrow, 2 * GW, WIDTH), (v, narrow, 2 * GW + WIDTH, WIDTH)):
            pltpu.make_async_copy(src.at[:, cols], xb.at[n, :, pl.ds(low, size)], in_sem.at[n]).start()
    for i, src in enumerate((pk, pv)):
        pltpu.make_async_copy(src, pkv.at[i], own_sem.at[2]).start()
    me.barrier()
    pltpu.make_async_copy(pkv, pkv, own_sem.at[2]).wait()

    for n, (head, there, device) in enumerate(routes):
        narrow = pl.ds(pl.multiple_of(head * WIDTH, WIDTH), WIDTH)
        on_y = head // SIDE
        piece, part = me.y * (1 - on_y) + me.x * on_y, me.x * (1 - on_y) + me.y * on_y
        src, dst = pkv.at[:, :, narrow], kv.at[me.z, piece, part, :, core_rows(me.c)]
        if device is None:
            pltpu.make_async_copy(src, dst, own_sem.at[1]).start()
        else:
            remote(src, dst, a_send.at[n], a_recv.at[there], device).start()

    row, slot = pack_rows(len_ref, prm_ref)
    pack = one_hot_pack(row)
    slot8 = jnp.broadcast_to(slot, (8, TOKENS)).astype(F32).astype(BF16)
    slot_send[...] = dot(slot8, pack, NT)
    for n, (_, there, device) in enumerate(routes):
        if device is None:
            pltpu.make_async_copy(slot_send, slots.at[there], own_sem.at[3]).start()
        else:
            remote(slot_send, slots.at[there], sl_send.at[n], sl_recv.at[there], device).start()

    def pack_rows_of(n):
        _, there, device = routes[n]
        pltpu.make_async_copy(xb.at[n], xb.at[n], in_sem.at[n]).wait()
        rows = dot(pack, xb[n], NN).astype(BF16)
        if device is None:
            recv[there] = rows
        else:
            send[n] = rows

    def send_rows(n):
        _, there, device = routes[n]
        if device is not None:
            remote(send.at[n], recv.at[there], x_send.at[n], x_recv.at[there], device).start()

    def pass_on(offset, ahead, sem, device):
        ref = kv.at[plane_of(ahead), piece_of(offset)]
        await_recv(ref, sem.at[offset])
        remote(ref, ref, f_send.at[offset], f_recv.at[offset], device).start()

    def spread(offset):
        ref = kv.at[me.z, piece_of(offset)]
        remote(ref, ref, cp_send.at[offset], cp_recv.at[offset], after).start()
        remote(ref, ref, cm_send.at[offset], cm_recv.at[offset], before).start()

    pack_rows_of(0)
    for n in range(EARLY):
        send_rows(n)
        pack_rows_of(n + 1)
    for k in range(SIDE):
        for core in (0, 1):
            there, _ = me.source(k, core)
            dst = kv.at[me.z, me.line, there // 2, :, core_rows(core)]
            if k == 0:
                pl.when(me.c == core)(lambda dst=dst: pltpu.make_async_copy(dst, dst, own_sem.at[1]).wait())
                pl.when(me.c != core)(lambda dst=dst, there=there: await_recv(dst, a_recv.at[there]))
            else:
                await_recv(dst, a_recv.at[there])
    for k in (1, 3, 2):
        ref = kv.at[me.z, me.line]
        remote(ref, ref, b_send.at[k - 1], b_recv.at[k - 1], me.line_peer(k)).start()
    spread(0)
    for n in range(EARLY, 4):
        if n > EARLY:
            pack_rows_of(n)
        send_rows(n)
    for k in (1, 3, 2):
        await_recv(kv.at[me.z, piece_of(k)], b_recv.at[SIDE - k - 1])
        spread(k)
        if k == 1:
            pass_on(0, 3, cp_recv, after)
        n = {1: 4, 3: 5, 2: 6}[k]
        pack_rows_of(n)
        send_rows(n)
    pack_rows_of(7)
    pass_on(1, 3, cp_recv, after)
    pass_on(3, 1, cm_recv, before)
    pass_on(2, 1, cm_recv, before)
    def one_hot(i):
        slot = slots[i][0:1].astype(jnp.int32)
        return jnp.where(lax.broadcasted_iota(jnp.int32, (TOKENS, LIVE), 0) == slot, 1.0, 0.0).astype(BF16)

    pltpu.make_async_copy(slot_send, slots.at[me.home_slot], own_sem.at[3]).wait()

    def unpack(m, carry):
        ahead = 2 + m // 2 + m // 4 + 2 * (m // 6)
        there = 2 * ((me.home_slot // 2 + ahead) % SIDE) + m % 2

        @pl.when(there != me.home_slot)
        def _():
            await_recv(slots.at[there], sl_recv.at[there])
            await_recv(recv.at[there], x_recv.at[there])

        rows = dot(one_hot(there), recv[there], NN).astype(BF16)
        xu[:, pl.ds(pl.multiple_of(there * SLOTS, SLOTS), SLOTS), :] = rows.reshape(RESPONSES, SLOTS, MSG)
        return carry

    lax.fori_loop(0, 8, unpack, 0)
    own_rows = lax.broadcasted_iota(jnp.int32, (WIDTH, WIDTH), 0)
    own_cols = lax.broadcasted_iota(jnp.int32, (WIDTH, WIDTH), 1)
    own_mask = (own_rows >> 4 == own_cols >> 4) & (own_cols <= own_rows)
    own_mask = jnp.concatenate([own_mask] * GROUP, axis=0)
    c = me.c

    def prompt(gz, gy):
        number = gy * SIDE + gz

        def chunk(i, quarter):
            return gz, gy * (1 - c) + quarter * c, quarter * (1 - c) + gy * c, i

        def heads(low):
            return jnp.concatenate([xu[number, :, low + a * WIDTH : low + (a + 1) * WIDTH] for a in range(GROUP)], axis=0)

        def put(low, rows):
            ou[:, gz, pl.ds(pl.multiple_of(gy * SLOTS, SLOTS), SLOTS), low : low + WIDTH] = rows.reshape(8, SLOTS, WIDTH)

        queries, grad_rows = heads(0), heads(GW)
        keys = jnp.concatenate([kv[chunk(0, i)] for i in range(SIDE)] + [xu[number, :, 2 * GW : 2 * GW + WIDTH]], axis=0)
        values = jnp.concatenate([kv[chunk(1, i)] for i in range(SIDE)] + [xu[number, :, 2 * GW + WIDTH :]], axis=0)
        scores = dot(queries, keys, NT)
        scores = jnp.concatenate([scores[:, :PREFIX], jnp.where(own_mask, scores[:, PREFIX:], -1e30)], axis=1)
        top = jnp.max(scores, axis=1, keepdims=True)
        weights = jnp.exp2((scores - top) * EXP2_SCALE)
        over = 1.0 / jnp.sum(weights, axis=1, keepdims=True)
        half = weights.astype(BF16)
        out = dot(half, values, NN) * over
        scaled = (grad_rows.astype(F32) * over).astype(BF16)
        row_dot = jnp.sum(scaled.astype(F32) * out, axis=1, keepdims=True)
        score_grad = (weights * (dot(scaled, values, NT) - row_dot)).astype(BF16)
        query_grad = dot(score_grad, keys, NN) * SCALE
        key_grad = (dot(score_grad, queries, TN) * SCALE).astype(BF16)
        value_grad = dot(half, scaled, TN).astype(BF16)
        dkv[gz, gy, 0] = key_grad[:PREFIX]
        dkv[gz, gy, 1] = value_grad[:PREFIX]
        for a in range(GROUP):
            put(a * WIDTH, out[a * WIDTH : (a + 1) * WIDTH].astype(BF16))
            put(GW + a * WIDTH, query_grad[a * WIDTH : (a + 1) * WIDTH].astype(BF16))
        put(2 * GW, key_grad[PREFIX:])
        put(2 * GW + WIDTH, value_grad[PREFIX:])

    def send_back(gz, gy):
        rows = pl.ds(pl.multiple_of(gy * SLOTS, SLOTS), SLOTS)
        for k in (2, 1, 3, 0):
            for core in (0, 1):
                there, device = me.source(k, core)
                index = 2 * k + core
                src, dst = ou.at[there, gz, rows], back.at[me.head, gz, rows]
                away = lambda: remote(src, dst, r_send.at[index], r_recv.at[me.head], device).start()
                if k == 0:
                    pl.when(c == core)(lambda: pltpu.make_async_copy(src, dst, own_sem.at[0]).start())
                    pl.when(c != core)(away)
                else:
                    away()

    def plan(n):
        quarter, odd = n // 4, n % 2
        first, middle = 1 - (quarter + 3) // 4, (quarter * (3 - quarter)) // 2
        ahead = first * 2 + middle * (1 + 2 * odd)
        gy = first * (odd * 2 + n // 2) + middle * (((n + 4) // 2 + 2 * (1 - odd)) % SIDE) + (1 - first - middle) * (n % SIDE)
        return (me.z + ahead) % SIDE, gy

    def step(count, carry):
        n = (count + SHIFT) % RESPONSES
        gz, gy = plan(n)

        @pl.when(n == 0)
        def _():
            for offset in (0, 3, 1, 2):
                await_recv(kv.at[plane_of(2), piece_of(offset)], f_recv.at[offset])

        @pl.when(n == 4)
        def _():
            for offset in (0, 1):
                await_recv(kv.at[plane_of(1), piece_of(offset)], cm_recv.at[offset])
            for offset in (3, 2):
                await_recv(kv.at[plane_of(3), piece_of(offset)], cp_recv.at[offset])

        prompt(gz, gy)

        @pl.when((n >= 8) & (n < 12))
        def _():
            await_recv(half_sum.at[gy], h_recv.at[gy])
            dkv[gz, gy] = (dkv[gz, gy].astype(F32) + half_sum[gy].astype(F32)).astype(BF16)

        for odd, device, got, send_sem, recv_sem in ((0, after, got_m, gm_send, gm_recv), (1, before, got_p, gp_send, gp_recv)):

            @pl.when((n < 4) & (n % 2 == odd))
            def _():
                remote(dkv.at[gz, gy], half_sum.at[gy], h_send.at[gy], h_recv.at[gy], device).start()

            @pl.when((n >= 4) & (n < 12) & (n % 2 == odd))
            def _():
                remote(dkv.at[gz, gy], got.at[gy], send_sem.at[gy], recv_sem.at[gy], device).start()

        @pl.when(count < HOLD)
        def _():
            send_back(gz, gy)

        return carry

    lax.fori_loop(0, RESPONSES, step, 0)

    def add_up(gy, carry):
        await_recv(got_m.at[gy], gm_recv.at[gy])
        await_recv(got_p.at[gy], gp_recv.at[gy])
        total = dkv[me.z, gy].astype(F32) + got_m[gy].astype(F32) + got_p[gy].astype(F32)
        plane_sum[gy] = total.astype(BF16)
        return carry

    lax.fori_loop(0, SIDE, add_up, 0)

    def columns(k):
        return pl.ds(pl.multiple_of((me.x + k) % SIDE * 96, 16), 96)

    @pl.when(c == 0)
    def _():
        for k in (2, 1, 3):
            remote(plane_sum.at[(me.y + k) % SIDE], got_y.at[k - 1], d_send.at[k - 1], d_recv.at[k - 1], me.line_peer(k)).start()

    @pl.when(c != 0)
    def _():
        for k in (2, 1, 3):
            remote(plane_sum.at[:, :, columns(k)], got_x.at[k - 1], d_send.at[k - 1], d_recv.at[k - 1], me.line_peer(k)).start()

    def late(n, carry):
        send_back(*plan((n + SHIFT) % RESPONSES))
        return carry

    lax.fori_loop(HOLD, RESPONSES, late, 0)

    def send_grads(part):
        for k in (2, 1, 3, 0):
            for core in (0, 1):
                _, device = me.source(k, core)
                index = 2 * k + core
                src, dst = part(k, core), grads.at[me.head]
                if k > 0 or core == 1 - part.core:
                    remote(src, dst, e_send.at[index], e_recv.at[me.head], device).start()
                else:
                    pltpu.make_async_copy(src, dst, own_sem.at[1]).start()

    @pl.when(c == 0)
    def _():
        total = plane_sum[me.y].astype(F32)
        for k in (1, 3, 2):
            await_recv(got_y.at[k - 1], d_recv.at[k - 1])
            total = total + got_y[k - 1].astype(F32)
        final_y[...] = total.astype(BF16)

        def part(k, core):
            return final_y.at[:, pl.ds(pl.multiple_of((2 * ((me.x + k) % SIDE) + core) * ROWS, 16), ROWS)]

        part.core = 0
        send_grads(part)

    @pl.when(c != 0)
    def _():
        total = plane_sum[:, :, columns(0)].astype(F32)
        for k in (1, 3, 2):
            await_recv(got_x.at[k - 1], d_recv.at[k - 1])
            total = total + got_x[k - 1].astype(F32)
        final_x[...] = total.astype(BF16)

        def part(k, core):
            return final_x.at[(me.y + k) % SIDE, :, pl.ds(core * ROWS, ROWS)]

        part.core = 1
        send_grads(part)

    for head, _, device in routes:
        if device is None:
            pltpu.make_async_copy(back.at[head], back.at[head], own_sem.at[0]).wait()
            pltpu.make_async_copy(grads.at[head], grads.at[head], own_sem.at[1]).wait()
        else:
            await_recv(back.at[head], r_recv.at[head])
            await_recv(grads.at[head], e_recv.at[head])
    for n in range(7):
        await_send(send.at[n], x_send.at[n])
        await_send(slot_send, sl_send.at[n])
        await_send(grads.at[0], a_send.at[n])
    for k in range(3):
        await_send(got_y.at[k], b_send.at[k])
        await_send(got_y.at[k], d_send.at[k])
    for offset in range(SIDE):
        for sem in (cp_send, cm_send, f_send, h_send, gm_send, gp_send):
            await_send(got_m.at[offset], sem.at[offset])

    def sent_back(index):
        await_send(back.at[0], r_send.at[index])
        await_send(grads.at[0], e_send.at[index])

    for index in range(8):
        if index < 2:
            pl.when(c != index)(lambda: sent_back(index))
        else:
            sent_back(index)


def place_kernel(len_ref, prm_ref, *refs):
    blocks, (grads, attn, query, key, value, prefix_key, prefix_value) = refs[:BATCH], refs[BATCH:]
    step = pl.program_id(0)
    token = lax.broadcasted_iota(jnp.int32, (SLOTS, GW), 0)
    for m, block in enumerate(blocks):
        live = token < len_ref[step * BATCH + m]
        rows = slice(m * SLOTS, (m + 1) * SLOTS)
        for h in range(KEY_HEADS):
            attn[rows, h * GW : (h + 1) * GW] = jnp.where(live, block[h, 0, :, :GW], jnp.zeros((), BF16))
            query[rows, h * GW : (h + 1) * GW] = block[h, 0, :, GW : 2 * GW]
            key[rows, h * WIDTH : (h + 1) * WIDTH] = block[h, 0, :, 2 * GW : 2 * GW + WIDTH]
            value[rows, h * WIDTH : (h + 1) * WIDTH] = block[h, 0, :, 2 * GW + WIDTH :]

    @pl.when(step == 0)
    def _():
        for h in range(KEY_HEADS):
            prefix_key[:, h * WIDTH : (h + 1) * WIDTH] = grads[h, 0].astype(F32)
            prefix_value[:, h * WIDTH : (h + 1) * WIDTH] = grads[h, 1].astype(F32)


def spec(space):
    return pl.BlockSpec(memory_space=space)


DMA = pltpu.SemaphoreType.DMA


def local(queries, grad_out, response_keys, response_values, prompt_prefix_keys, prompt_prefix_values, lengths, prompt_of):
    q, g = queries.reshape(TOKENS, KEY_HEADS * GW), grad_out.reshape(TOKENS, KEY_HEADS * GW)
    k, v = response_keys.reshape(TOKENS, KEY_HEADS * WIDTH), response_values.reshape(TOKENS, KEY_HEADS * WIDTH)
    pk, pv = prompt_prefix_keys.reshape(ROWS, KEY_HEADS * WIDTH), prompt_prefix_values.reshape(ROWS, KEY_HEADS * WIDTH)
    lens, prompts = lengths.reshape(RESPONSES), prompt_of.reshape(RESPONSES)
    vmem = pltpu.VMEM
    back, grads = pl.pallas_call(
        main_kernel,
        out_shape=(
            jax.ShapeDtypeStruct((8, SIDE, SIDE * SLOTS, MSG), BF16),
            jax.ShapeDtypeStruct((8, 2, ROWS, WIDTH), BF16),
        ),
        in_specs=[spec(pltpu.SMEM)] * 2 + [spec(pl.ANY)] * 6,
        out_specs=(spec(pl.ANY),) * 2,
        scratch_shapes=[
            vmem((8, TOKENS, MSG), BF16), vmem((7, LIVE, MSG), BF16), vmem((8, LIVE), F32),
            vmem((8, LIVE, MSG), BF16), vmem((8, 8, LIVE), F32), vmem((SIDE, SIDE, SIDE, 2, 96, WIDTH), BF16),
            vmem((2, ROWS, KEY_HEADS * WIDTH), BF16),
            vmem((RESPONSES, 8 * SLOTS, MSG), BF16), vmem((8, SIDE, SIDE * SLOTS, MSG), BF16),
            vmem((SIDE, SIDE, 2, PREFIX, WIDTH), BF16), vmem((SIDE, 2, PREFIX, WIDTH), BF16), vmem((SIDE, 2, PREFIX, WIDTH), BF16),
            vmem((SIDE, 2, PREFIX, WIDTH), BF16), vmem((SIDE, 2, PREFIX, WIDTH), BF16),
            vmem((3, 2, PREFIX, WIDTH), BF16), vmem((3, SIDE, 2, 96, WIDTH), BF16),
            vmem((2, PREFIX, WIDTH), BF16), vmem((SIDE, 2, 96, WIDTH), BF16),
            DMA((8,)), DMA((8,)), DMA((8,)), DMA((8,)), DMA((8,)), DMA((8,)), DMA((8,)), DMA((3,)), DMA((3,)),
        ] + [DMA((SIDE,))] * 12 + [DMA((3,)), DMA((3,)), DMA((8,)), DMA((8,)), DMA((8,)), DMA((8,)), DMA((4,))],
        compiler_params=pltpu.CompilerParams(collective_id=0, has_side_effects=True, vmem_limit_bytes=VMEM_LIMIT),
    )(lens, prompts, q, g, k, v, pk, pv)
    def block_of(m):
        def index(i, lens, prompts):
            there = prompts[i * BATCH + m]
            return 0, there % SIDE, there // SIDE, 0

        return pl.BlockSpec((KEY_HEADS, 1, SLOTS, MSG), index)

    wide = pl.BlockSpec((BATCH * SLOTS, KEY_HEADS * GW), lambda i, *_: (i, 0))
    narrow = pl.BlockSpec((BATCH * SLOTS, KEY_HEADS * WIDTH), lambda i, *_: (i, 0))
    prefix = pl.BlockSpec((ROWS, KEY_HEADS * WIDTH), lambda i, *_: (0, 0))
    outs = pl.pallas_call(
        place_kernel,
        grid_spec=pltpu.PrefetchScalarGridSpec(
            num_scalar_prefetch=2,
            grid=(RESPONSES // BATCH,),
            in_specs=[block_of(m) for m in range(BATCH)] + [pl.BlockSpec(grads.shape, lambda i, *_: (0, 0, 0, 0))],
            out_specs=[wide, wide, narrow, narrow, prefix, prefix],
        ),
        out_shape=[
            jax.ShapeDtypeStruct(q.shape, BF16),
            jax.ShapeDtypeStruct(q.shape, BF16),
            jax.ShapeDtypeStruct(k.shape, BF16),
            jax.ShapeDtypeStruct(k.shape, BF16),
            jax.ShapeDtypeStruct(pk.shape, F32),
            jax.ShapeDtypeStruct(pk.shape, F32),
        ],
        compiler_params=pltpu.CompilerParams(vmem_limit_bytes=VMEM_LIMIT),
    )(lens, prompts, *[back] * BATCH, grads)
    shapes = (queries, queries, response_keys, response_keys, prompt_prefix_keys, prompt_prefix_keys)
    return tuple(out.reshape(like.shape) for out, like in zip(outs, shapes))


def solution(mesh):
    five, three = P("prompt", "resp", None, None, None), P("prompt", "resp", None)
    return jax.shard_map(
        local,
        mesh=mesh,
        in_specs=(five, five, five, five, three, three, three, three),
        out_specs=(five, five, five, five, three, three),
        check_vma=False,
    )
```

time: 110 us -> 100 us (0.909)
  the two profiles are of different devices: /device:TPU:1 before, /device:TPU:11 now
where the time goes in v2:
time: 100 us
  Pallas kernels  99.6 us (100%)
    pallas_call x1, Pallas kernels, local(): pl.pallas_call(main_kernel, out_shape=(jax.ShapeDtypeStruct((8, SIDE, SID...  92.7 us
    pallas_call x1, Pallas kernels, local(): pl.pallas_call(place_kernel, grid_spec=pltpu.PrefetchScalarGridSpec(num_s...  6.9 us

profile of v2, /device:TPU:11, one launch (start us, length us, event | category | flops | bytes accessed | tf_op | source)
XLA Modules:
  0.0 100.2 jit_solution(6216984608921316159)
XLA Ops:
  0.6 92.7 %shard_map.127 = (bf16[8,4,64,1536]{3,2,1,0:T(8,128)(2,1)}, bf16[8,2,48,128]{3,2,1,0:T(8,128)(2,1)}) custom-call(s32[16]{0:T(128)} %bitcast.20, s32[16]{0:T(128)} %bitcast.22, bf16[256,5120]{1,0:T(8,128)(2,1)} %bitcast.14, bf16[256,5120]{1,0:T(8,128)(2,1)} %bitcast.15, bf16[256,1024]{1,0:T(8,128)(2,1)} %bitcast.16, bf16[256,1024]{1,0:T(8,128)(2,1)} %bitcast.17, ...), custom_call_target="tpu_custom_call" | custom-call | tf_op jit(solution)/shard_map/pallas_call | solution.py:474
  93.3 6.9 %shard_map.128 = (bf16[256,5120]{1,0:T(8,128)(2,1)}, bf16[256,5120]{1,0:T(8,128)(2,1)}, bf16[256,1024]{1,0:T(8,128)(2,1)}, bf16[256,1024]{1,0:T(8,128)(2,1)}, f32[48,1024]{1,0:T(8,128)}, /*index=5*/f32[48,1024]{1,0:T(8,128)}) custom-call(s32[16]{0:T(128)} %bitcast.21, s32[16]{0:T(128)} %bitcast.23, ...), custom_call_target="tpu_custom_call" | custom-call | tf_op jit(solution)/shard_map/pallas_call | solution.py:505

commit v3 on v2

--- a/solution.py
+++ b/solution.py
@@ -22,9 +22,9 @@
 F32 = jnp.float32
 SCALE = WIDTH**-0.5
 EXP2_SCALE = SCALE * 1.4426950408889634
-BATCH = 4
+BATCH = 8
 HOLD = 14
-EARLY = 0
+FIRST = 2
 SHIFT = 0
 VMEM_LIMIT = 58 * 1024 * 1024
 
@@ -58,6 +58,17 @@
         prompt = ((self.y + k * (1 - self.c)) % SIDE) * SIDE + self.z
         return (prompt, ((self.x + k * self.c) % SIDE) * 2 + self.c)
 
+    def beside(self, n, k):
+        x, y, z, c = self.x, self.y, self.z, self.c
+        if n == 7:
+            return self.line_peer(k)
+        if n == 6:
+            return (((y + k * c) % SIDE) * SIDE + z, ((x + k * (1 - c)) % SIDE) * 2 + 1 - c)
+        ahead = (2, 1, 3)[n // 2]
+        if n % 2 == 0:
+            return (((y + k) % SIDE) * SIDE + z, 2 * ((x + ahead) % SIDE))
+        return (((y + ahead) % SIDE) * SIDE + z, 2 * ((x + k) % SIDE) + 1)
+
     def z_peer(self, k):
         return (self.y * SIDE + (self.z + k) % SIDE, self.resp)
 
@@ -69,6 +80,8 @@
             for core in (0, 1):
                 peers.append((self.prompt, ((self.x + k) % SIDE) * 2 + core))
                 peers.append((((self.y + k) % SIDE) * SIDE + self.z, 2 * self.x + core))
+                for j in (1, 2, 3):
+                    peers.append((((self.y + k) % SIDE) * SIDE + self.z, ((self.x + j) % SIDE) * 2 + core))
         for peer in peers:
             pl.semaphore_signal(sem, inc=1, device_id=peer, device_id_type=MESH)
         pl.semaphore_wait(sem, len(peers))
@@ -137,19 +150,22 @@
         for src, cols, low, size in ((q, wide, 0, GW), (g, wide, GW, GW), (k, narrow, 2 * GW, WIDTH), (v, narrow, 2 * GW + WIDTH, WIDTH)):
             pltpu.make_async_copy(src.at[:, cols], xb.at[n, :, pl.ds(low, size)], in_sem.at[n]).start()
     for i, src in enumerate((pk, pv)):
-        pltpu.make_async_copy(src, pkv.at[i], own_sem.at[2]).start()
+        for h in range(KEY_HEADS):
+            pltpu.make_async_copy(src.at[:, pl.ds(h * WIDTH, WIDTH)], pkv.at[h, i], own_sem.at[2]).start()
     me.barrier()
     pltpu.make_async_copy(pkv, pkv, own_sem.at[2]).wait()
 
-    for n, (head, there, device) in enumerate(routes):
-        narrow = pl.ds(pl.multiple_of(head * WIDTH, WIDTH), WIDTH)
-        on_y = head // SIDE
-        piece, part = me.y * (1 - on_y) + me.x * on_y, me.x * (1 - on_y) + me.y * on_y
-        src, dst = pkv.at[:, :, narrow], kv.at[me.z, piece, part, :, core_rows(me.c)]
-        if device is None:
-            pltpu.make_async_copy(src, dst, own_sem.at[1]).start()
-        else:
-            remote(src, dst, a_send.at[n], a_recv.at[there], device).start()
+    for k in (0, 1, 3, 2):
+        for n, (head, there, device) in enumerate(routes):
+            on_y = head // SIDE
+            piece, part = me.y * (1 - on_y) + me.x * on_y, me.x * (1 - on_y) + me.y * on_y
+            src, dst = pkv.at[head], kv.at[me.z, piece, part, :, core_rows(me.c)]
+            if k > 0:
+                remote(src, dst, b_send.at[k - 1], b_recv.at[k - 1], me.beside(n, k)).start()
+            elif device is None:
+                pltpu.make_async_copy(src, dst, own_sem.at[1]).start()
+            else:
+                remote(src, dst, a_send.at[n], a_recv.at[there], device).start()
 
     row, slot = pack_rows(len_ref, prm_ref)
     pack = one_hot_pack(row)
@@ -185,10 +201,9 @@
         remote(ref, ref, cp_send.at[offset], cp_recv.at[offset], after).start()
         remote(ref, ref, cm_send.at[offset], cm_recv.at[offset], before).start()
 
-    pack_rows_of(0)
-    for n in range(EARLY):
+    for n in range(FIRST):
+        pack_rows_of(n)
         send_rows(n)
-        pack_rows_of(n + 1)
     for k in range(SIDE):
         for core in (0, 1):
             there, _ = me.source(k, core)
@@ -198,23 +213,18 @@
                 pl.when(me.c != core)(lambda dst=dst, there=there: await_recv(dst, a_recv.at[there]))
             else:
                 await_recv(dst, a_recv.at[there])
-    for k in (1, 3, 2):
-        ref = kv.at[me.z, me.line]
-        remote(ref, ref, b_send.at[k - 1], b_recv.at[k - 1], me.line_peer(k)).start()
     spread(0)
-    for n in range(EARLY, 4):
-        if n > EARLY:
-            pack_rows_of(n)
+    for n in range(FIRST, 4):
+        pack_rows_of(n)
         send_rows(n)
     for k in (1, 3, 2):
         await_recv(kv.at[me.z, piece_of(k)], b_recv.at[SIDE - k - 1])
         spread(k)
-        if k == 1:
-            pass_on(0, 3, cp_recv, after)
         n = {1: 4, 3: 5, 2: 6}[k]
         pack_rows_of(n)
         send_rows(n)
     pack_rows_of(7)
+    pass_on(0, 3, cp_recv, after)
     pass_on(1, 3, cp_recv, after)
     pass_on(3, 1, cm_recv, before)
     pass_on(2, 1, cm_recv, before)
@@ -482,7 +492,7 @@
         scratch_shapes=[
             vmem((8, TOKENS, MSG), BF16), vmem((7, LIVE, MSG), BF16), vmem((8, LIVE), F32),
             vmem((8, LIVE, MSG), BF16), vmem((8, 8, LIVE), F32), vmem((SIDE, SIDE, SIDE, 2, 96, WIDTH), BF16),
-            vmem((2, ROWS, KEY_HEADS * WIDTH), BF16),
+            vmem((KEY_HEADS, 2, ROWS, WIDTH), BF16),
             vmem((RESPONSES, 8 * SLOTS, MSG), BF16), vmem((8, SIDE, SIDE * SLOTS, MSG), BF16),
             vmem((SIDE, SIDE, 2, PREFIX, WIDTH), BF16), vmem((SIDE, 2, PREFIX, WIDTH), BF16), vmem((SIDE, 2, PREFIX, WIDTH), BF16),
             vmem((SIDE, 2, PREFIX, WIDTH), BF16), vmem((SIDE, 2, PREFIX, WIDTH), BF16),

time: 100 us -> 96.6 us (0.966)
  the two profiles are of different devices: /device:TPU:11 before, /device:TPU:1 now
where the time goes in v3:
time: 96.6 us; the launch traced here: 96.5 us
  Pallas kernels  95.8 us (99%)
    pallas_call x1, Pallas kernels, local(): pl.pallas_call(main_kernel, out_shape=(jax.ShapeDtypeStruct((8, SIDE, SID...  89.9 us
    pallas_call x1, Pallas kernels, local(): pl.pallas_call(place_kernel, grid_spec=pltpu.PrefetchScalarGridSpec(num_s...  5.94 us

profile of v3, /device:TPU:1, one launch (start us, length us, event | category | flops | bytes accessed | tf_op | source)
XLA Modules:
  0.0 96.5 jit_solution(15912853155757239951)
XLA Ops:
  0.6 89.9 %shard_map.127 = (bf16[8,4,64,1536]{3,2,1,0:T(8,128)(2,1)}, bf16[8,2,48,128]{3,2,1,0:T(8,128)(2,1)}) custom-call(s32[16]{0:T(128)} %bitcast.20, s32[16]{0:T(128)} %bitcast.22, bf16[256,5120]{1,0:T(8,128)(2,1)} %bitcast.14, bf16[256,5120]{1,0:T(8,128)(2,1)} %bitcast.15, bf16[256,1024]{1,0:T(8,128)(2,1)} %bitcast.16, bf16[256,1024]{1,0:T(8,128)(2,1)} %bitcast.17, ...), custom_call_target="tpu_custom_call" | custom-call | tf_op jit(solution)/shard_map/pallas_call | solution.py:484
  90.5 5.9 %shard_map.128 = (bf16[256,5120]{1,0:T(8,128)(2,1)}, bf16[256,5120]{1,0:T(8,128)(2,1)}, bf16[256,1024]{1,0:T(8,128)(2,1)}, bf16[256,1024]{1,0:T(8,128)(2,1)}, f32[48,1024]{1,0:T(8,128)}, /*index=5*/f32[48,1024]{1,0:T(8,128)}) custom-call(s32[16]{0:T(128)} %bitcast.21, s32[16]{0:T(128)} %bitcast.23, ...), custom_call_target="tpu_custom_call" | custom-call | tf_op jit(solution)/shard_map/pallas_call | solution.py:515

commit v4 on v3

--- a/solution.py
+++ b/solution.py
@@ -25,6 +25,8 @@
 BATCH = 8
 HOLD = 14
 FIRST = 2
+LOW, HIGH, BOTH = pl.ds(0, 2), pl.ds(2, 2), pl.ds(0, 4)
+PASSED = ((0, LOW), (0, HIGH), (1, BOTH), (3, BOTH), (2, LOW), (2, HIGH))
 SHIFT = 0
 VMEM_LIMIT = 58 * 1024 * 1024
 
@@ -191,10 +193,11 @@
         if device is not None:
             remote(send.at[n], recv.at[there], x_send.at[n], x_recv.at[there], device).start()
 
-    def pass_on(offset, ahead, sem, device):
-        ref = kv.at[plane_of(ahead), piece_of(offset)]
-        await_recv(ref, sem.at[offset])
-        remote(ref, ref, f_send.at[offset], f_recv.at[offset], device).start()
+    def pass_on(offset, index, parts, forward):
+        ref = kv.at[plane_of(3 if forward else 1), piece_of(offset)]
+        await_recv(ref, (cp_recv if forward else cm_recv).at[offset])
+        ref = ref.at[parts]
+        remote(ref, ref, f_send.at[index], f_recv.at[index], after if forward else before).start()
 
     def spread(offset):
         ref = kv.at[me.z, piece_of(offset)]
@@ -217,6 +220,8 @@
     for n in range(FIRST, 4):
         pack_rows_of(n)
         send_rows(n)
+    pass_on(0, 0, LOW, True)
+    pass_on(0, 1, HIGH, False)
     for k in (1, 3, 2):
         await_recv(kv.at[me.z, piece_of(k)], b_recv.at[SIDE - k - 1])
         spread(k)
@@ -224,10 +229,11 @@
         pack_rows_of(n)
         send_rows(n)
     pack_rows_of(7)
-    pass_on(0, 3, cp_recv, after)
-    pass_on(1, 3, cp_recv, after)
-    pass_on(3, 1, cm_recv, before)
-    pass_on(2, 1, cm_recv, before)
+    pass_on(1, 2, BOTH, True)
+    pass_on(3, 3, BOTH, False)
+    pass_on(2, 4, LOW, True)
+    pass_on(2, 5, HIGH, False)
+
     def one_hot(i):
         slot = slots[i][0:1].astype(jnp.int32)
         return jnp.where(lax.broadcasted_iota(jnp.int32, (TOKENS, LIVE), 0) == slot, 1.0, 0.0).astype(BF16)
@@ -317,15 +323,13 @@
 
         @pl.when(n == 0)
         def _():
-            for offset in (0, 3, 1, 2):
-                await_recv(kv.at[plane_of(2), piece_of(offset)], f_recv.at[offset])
+            for index, (offset, parts) in enumerate(PASSED):
+                await_recv(kv.at[plane_of(2), piece_of(offset), parts], f_recv.at[index])
 
         @pl.when(n == 4)
         def _():
-            for offset in (0, 1):
-                await_recv(kv.at[plane_of(1), piece_of(offset)], cm_recv.at[offset])
-            for offset in (3, 2):
-                await_recv(kv.at[plane_of(3), piece_of(offset)], cp_recv.at[offset])
+            await_recv(kv.at[plane_of(1), piece_of(1)], cm_recv.at[1])
+            await_recv(kv.at[plane_of(3), piece_of(3)], cp_recv.at[3])
 
         prompt(gz, gy)
 
@@ -434,8 +438,11 @@
         await_send(got_y.at[k], b_send.at[k])
         await_send(got_y.at[k], d_send.at[k])
     for offset in range(SIDE):
-        for sem in (cp_send, cm_send, f_send, h_send, gm_send, gp_send):
+        for sem in (cp_send, cm_send, h_send, gm_send, gp_send):
             await_send(got_m.at[offset], sem.at[offset])
+
+    for index, (_, parts) in enumerate(PASSED):
+        await_send(kv.at[0, 0, parts], f_send.at[index])
 
     def sent_back(index):
         await_send(back.at[0], r_send.at[index])
@@ -499,7 +506,7 @@
             vmem((3, 2, PREFIX, WIDTH), BF16), vmem((3, SIDE, 2, 96, WIDTH), BF16),
             vmem((2, PREFIX, WIDTH), BF16), vmem((SIDE, 2, 96, WIDTH), BF16),
             DMA((8,)), DMA((8,)), DMA((8,)), DMA((8,)), DMA((8,)), DMA((8,)), DMA((8,)), DMA((3,)), DMA((3,)),
-        ] + [DMA((SIDE,))] * 12 + [DMA((3,)), DMA((3,)), DMA((8,)), DMA((8,)), DMA((8,)), DMA((8,)), DMA((4,))],
+        ] + [DMA((SIDE,))] * 4 + [DMA((6,))] * 2 + [DMA((SIDE,))] * 6 + [DMA((3,)), DMA((3,)), DMA((8,)), DMA((8,)), DMA((8,)), DMA((8,)), DMA((4,))],
         compiler_params=pltpu.CompilerParams(collective_id=0, has_side_effects=True, vmem_limit_bytes=VMEM_LIMIT),
     )(lens, prompts, q, g, k, v, pk, pv)
     def block_of(m):

time: 96.6 us -> 96.5 us (level)
  no operation moved by 1% of the time
where the time goes in v4:
time: 96.5 us; the launch traced here: 96.4 us
  Pallas kernels  95.8 us (99%)
    pallas_call x1, Pallas kernels, local(): pl.pallas_call(main_kernel, out_shape=(jax.ShapeDtypeStruct((8, SIDE, SID...  89.8 us
    pallas_call x1, Pallas kernels, local(): pl.pallas_call(place_kernel, grid_spec=pltpu.PrefetchScalarGridSpec(num_s...  5.94 us

profile of v4, /device:TPU:1, one launch (start us, length us, event | category | flops | bytes accessed | tf_op | source)
XLA Modules:
  0.0 96.4 jit_solution(17168459189520375783)
XLA Ops:
  0.6 89.8 %shard_map.127 = (bf16[8,4,64,1536]{3,2,1,0:T(8,128)(2,1)}, bf16[8,2,48,128]{3,2,1,0:T(8,128)(2,1)}) custom-call(s32[16]{0:T(128)} %bitcast.20, s32[16]{0:T(128)} %bitcast.22, bf16[256,5120]{1,0:T(8,128)(2,1)} %bitcast.14, bf16[256,5120]{1,0:T(8,128)(2,1)} %bitcast.15, bf16[256,1024]{1,0:T(8,128)(2,1)} %bitcast.16, bf16[256,1024]{1,0:T(8,128)(2,1)} %bitcast.17, ...), custom_call_target="tpu_custom_call" | custom-call | tf_op jit(solution)/shard_map/pallas_call | solution.py:491
  90.5 5.9 %shard_map.128 = (bf16[256,5120]{1,0:T(8,128)(2,1)}, bf16[256,5120]{1,0:T(8,128)(2,1)}, bf16[256,1024]{1,0:T(8,128)(2,1)}, bf16[256,1024]{1,0:T(8,128)(2,1)}, f32[48,1024]{1,0:T(8,128)}, /*index=5*/f32[48,1024]{1,0:T(8,128)}) custom-call(s32[16]{0:T(128)} %bitcast.21, s32[16]{0:T(128)} %bitcast.23, ...), custom_call_target="tpu_custom_call" | custom-call | tf_op jit(solution)/shard_map/pallas_call | solution.py:522

commit v5 on v4

--- a/solution.py
+++ b/solution.py
@@ -157,7 +157,7 @@
     me.barrier()
     pltpu.make_async_copy(pkv, pkv, own_sem.at[2]).wait()
 
-    for k in (0, 1, 3, 2):
+    for k in (0, 1, 3):
         for n, (head, there, device) in enumerate(routes):
             on_y = head // SIDE
             piece, part = me.y * (1 - on_y) + me.x * on_y, me.x * (1 - on_y) + me.y * on_y
@@ -216,6 +216,8 @@
                 pl.when(me.c != core)(lambda dst=dst, there=there: await_recv(dst, a_recv.at[there]))
             else:
                 await_recv(dst, a_recv.at[there])
+    ref = kv.at[me.z, me.line]
+    remote(ref, ref, b_send.at[1], b_recv.at[1], me.line_peer(2)).start()
     spread(0)
     for n in range(FIRST, 4):
         pack_rows_of(n)

time: 96.5 us -> 97.7 us (1.012)
  Pallas kernels: 95.8 us -> 96.9 us
    pallas_call x1, Pallas kernels: 89.8 us -> 90.9 us  [local(): pl.pallas_call(main_kernel, out_shape=(jax.ShapeDtypeStruct((8, SIDE, SID...]
where the time goes in v5:
time: 97.7 us; the launch traced here: 97.5 us
  Pallas kernels  96.9 us (99%)
    pallas_call x1, Pallas kernels, local(): pl.pallas_call(main_kernel, out_shape=(jax.ShapeDtypeStruct((8, SIDE, SID...  90.9 us
    pallas_call x1, Pallas kernels, local(): pl.pallas_call(place_kernel, grid_spec=pltpu.PrefetchScalarGridSpec(num_s...  5.94 us

profile of v5, /device:TPU:1, one launch (start us, length us, event | category | flops | bytes accessed | tf_op | source)
XLA Modules:
  0.0 97.5 jit_solution(1614341433524060281)
XLA Ops:
  0.6 90.9 %shard_map.127 = (bf16[8,4,64,1536]{3,2,1,0:T(8,128)(2,1)}, bf16[8,2,48,128]{3,2,1,0:T(8,128)(2,1)}) custom-call(s32[16]{0:T(128)} %bitcast.20, s32[16]{0:T(128)} %bitcast.22, bf16[256,5120]{1,0:T(8,128)(2,1)} %bitcast.14, bf16[256,5120]{1,0:T(8,128)(2,1)} %bitcast.15, bf16[256,1024]{1,0:T(8,128)(2,1)} %bitcast.16, bf16[256,1024]{1,0:T(8,128)(2,1)} %bitcast.17, ...), custom_call_target="tpu_custom_call" | custom-call | tf_op jit(solution)/shard_map/pallas_call | solution.py:493
  91.6 5.9 %shard_map.128 = (bf16[256,5120]{1,0:T(8,128)(2,1)}, bf16[256,5120]{1,0:T(8,128)(2,1)}, bf16[256,1024]{1,0:T(8,128)(2,1)}, bf16[256,1024]{1,0:T(8,128)(2,1)}, f32[48,1024]{1,0:T(8,128)}, /*index=5*/f32[48,1024]{1,0:T(8,128)}) custom-call(s32[16]{0:T(128)} %bitcast.21, s32[16]{0:T(128)} %bitcast.23, ...), custom_call_target="tpu_custom_call" | custom-call | tf_op jit(solution)/shard_map/pallas_call | solution.py:524
